TPU v7x, 128 devices: a whole 4x4x4 slice. The times are simulated.
128 devices in a mesh: tm: 64 (over z, x, y), blk: 2 (over core).
Axes of the slice: x: 4, y: 4, z: 4, core: 2. Of those that a mesh axis runs over, the one named last changes fastest.
Arguments:
- diag_blocks: float32 [128, 1024, 1024], P('tm', None, 'blk'), may hold values from -24 to 60, as said below
- sub_blocks: float32 [128, 1024, 1024], P('tm', None, 'blk'), may hold values from -17 to 2
- arrow_blocks: float32 [128, 64, 1024], P('tm', None, 'blk'), may hold values from -1 to 1
- tip_block: float32 [64, 64], replicated, may hold values from -2 to 14, as said below
Outputs:
- pivot_diag: float32 [64, 1024, 1024], P('tm', None, 'blk')
- pivot_left: float32 [64, 1024, 1024], P('tm', None, 'blk')
- pivot_arrow: float32 [64, 64, 1024], P('tm', None, 'blk')
- tip_schur: float32 [64, 64], replicated
- log_det: float32 [], replicated
Inputs may be any that keep to these rules, and one draw needn't show every extreme that they name: Every diag_blocks[s] is symmetric, and the slab part of Q (without the fixed-effect rows) is positive definite. tip_block is symmetric.
All inputs are finite; a program needn't handle non-finite values.
Results may differ from a plain program's by a relative error of at most 0.0003.
Values sent between devices are 32-bit elements; how exact they have to be, the bound alone decides.
A program may use at most 192 MiB of HBM per device.

v0:
```python
import functools

import jax
import jax.numpy as jnp
from jax import lax
from jax.experimental import pallas as pl
from jax.experimental.pallas import tpu as pltpu
from jax.sharding import PartitionSpec as P

F32 = jnp.float32
BF16 = jnp.bfloat16
TILE = 128
BLOCK = 256
PACKED = 5
COPIES = 4
GROUP = 2
SLOTS = TILE // (8 * GROUP)


def row_of(value, index):
    return jnp.broadcast_to(value[index : index + 1, :], (8, value.shape[1]))


def column_of(value, index):
    return jnp.broadcast_to(value[:, index : index + 1], (8, TILE))


def split_three(value):
    high = value.astype(BF16).astype(F32)
    rest = value - high
    middle = rest.astype(BF16).astype(F32)
    return high, middle, rest - middle


def split_two(value):
    high = value.astype(BF16)
    return high, (value - high.astype(F32)).astype(BF16)


def left_pieces(value):
    high, low = split_two(value)
    return jnp.concatenate([high, low, high], axis=1)


def right_pieces(value):
    high, low = split_two(value)
    return jnp.concatenate([high, high, low], axis=0)


def outer_product(rows_a, rows_b):
    ah, am, al = split_three(rows_a)
    bh, bm, bl = split_three(rows_b)
    left = jnp.concatenate([ah, am, ah, am, al, ah], axis=0).astype(BF16)
    right = jnp.concatenate([bh, bh, bm, bm, bh, bl], axis=0).astype(BF16)
    return lax.dot_general(left, right, (((0,), (0,)), ((), ())), preferred_element_type=F32)


def sweep_rows(rows, first, pivots, lane, sub):
    count = 8 * len(rows)
    columns = [[column_of(row, first + c) for c in range(count)] for row in rows]
    inside = (lane >= first) & (lane < first + count)
    solved = [
        jnp.where(lane == sub + first + 8 * h, -1.0, jnp.where(inside, 0.0, row)) for h, row in enumerate(rows)
    ]
    for c in range(count):
        group, place = c // 8, c % 8
        pivot = row_of(columns[group][c], place)
        scale = 1.0 / pivot
        pivots = jnp.where(lane == first + c, pivot, pivots)
        pivot_row = row_of(solved[group], place) * scale
        for h in range(len(rows)):
            value = solved[h] - columns[h][c] * pivot_row
            solved[h] = jnp.where(sub == place, pivot_row, value) if h == group else value
        for d in range(c + 1, count):
            entry = row_of(columns[group][d], place) * scale
            for h in range(len(rows)):
                value = columns[h][d] - columns[h][c] * entry
                columns[h][d] = jnp.where(sub == place, entry, value) if h == group else value
    return solved, pivots


def sweep_tile(tile, beside=None):
    lane = lax.broadcasted_iota(jnp.int32, (8, TILE), 1)
    sub = lax.broadcasted_iota(jnp.int32, (8, TILE), 0)
    pivots = jnp.ones((8, TILE), F32)
    width = 8 * GROUP
    rows = [tile[8 * i : 8 * i + 8, :] for i in range(TILE // 8)]
    for i in range(TILE // width):
        source = rows[GROUP * i : GROUP * i + GROUP]
        inside = (lane >= width * i) & (lane < width * i + width)
        solved, pivots = sweep_rows(source, width * i, pivots, lane, sub)
        update = outer_product(jnp.concatenate(source, axis=0), jnp.concatenate(solved, axis=0))
        for k in range(TILE // 8):
            if k // GROUP == i:
                continue
            kept = jnp.where(inside, 0.0, rows[k])
            if k == GROUP * (i + 1):
                for c in range(width):
                    kept = kept - column_of(rows[k], width * i + c) * row_of(solved[c // 8], c % 8)
                rows[k] = kept
            else:
                rows[k] = kept - update[8 * k : 8 * k + 8, :]
        rows[GROUP * i : GROUP * i + GROUP] = solved
        if beside is not None:
            beside(i)
    return jnp.concatenate(rows, axis=0), pivots


def tile_span(index):
    return pl.ds(pl.multiple_of(index * TILE, TILE), TILE)


def close_tile(order, matrix_ref, left_ref, swept_ref, tile_ref, j, swept):
    count = order // TILE
    here, there = tile_span(j), tile_span(lax.rem(j + 1, count))
    swept_ref[...] = swept
    solved = jnp.dot(left_pieces(swept), right_pieces(matrix_ref[here, there]), preferred_element_type=F32)
    tile_ref[...] = matrix_ref[there, there] + jnp.dot(
        left_pieces(matrix_ref[there, here]), right_pieces(solved), preferred_element_type=F32
    )
    matrix_ref[here, here] = jnp.zeros((TILE, TILE), F32)
    for r in range(count):
        span = slice(r * TILE, (r + 1) * TILE)
        left_ref[span, :] = left_pieces(matrix_ref[span, here])
    matrix_ref[:, here] = jnp.zeros((order, TILE), F32)
    matrix_ref[here, here] = swept


def solve_tile_rows(order, matrix_ref, swept_ref, right_ref, j):
    here = tile_span(j)
    rows = matrix_ref[here, :]
    lane = lax.broadcasted_iota(jnp.int32, (TILE, order), 1)
    inside = (lane >= j * TILE) & (lane < j * TILE + TILE)
    solved = -jnp.dot(left_pieces(swept_ref[...]), right_pieces(rows), preferred_element_type=F32)
    solved = jnp.where(inside, rows, solved)
    right_ref[...] = right_pieces(solved)
    matrix_ref[here, :] = solved


def update_rows(matrix_ref, left_ref, right_ref, span):
    matrix_ref[span, :] = matrix_ref[span, :] - jnp.dot(
        left_ref[span, :], right_ref[...], preferred_element_type=F32
    )


def eliminate_all(order, matrix_ref, log_ref, left_ref, right_ref, swept_ref, tile_ref):
    count = order // TILE
    swept, pivots = sweep_tile(matrix_ref[0:TILE, 0:TILE])
    close_tile(order, matrix_ref, left_ref, swept_ref, tile_ref, 0, swept)

    def step(j, logs):
        def beside(i):
            if i == 0:
                solve_tile_rows(order, matrix_ref, swept_ref, right_ref, j - 1)
                return
            first = (i - 1) * count // (SLOTS - 1)
            for r in range(first, i * count // (SLOTS - 1)):
                update_rows(matrix_ref, left_ref, right_ref, slice(r * TILE, (r + 1) * TILE))

        swept, pivots = sweep_tile(tile_ref[...], beside)
        close_tile(order, matrix_ref, left_ref, swept_ref, tile_ref, j, swept)
        return logs + jnp.log(pivots)

    log_ref[...] = lax.fori_loop(1, count, step, jnp.log(pivots))
    solve_tile_rows(order, matrix_ref, swept_ref, right_ref, count - 1)

    def update(r, carry):
        update_rows(matrix_ref, left_ref, right_ref, tile_span(r))
        return carry

    lax.fori_loop(0, count, update, 0)


def inverse_kernel(source_ref, inverse_ref, log_ref, *scratch):
    order = source_ref.shape[0]

    def take(r, carry):
        inverse_ref[tile_span(r), :] = source_ref[tile_span(r), :]
        return carry

    lax.fori_loop(0, order // TILE, take, 0)
    eliminate_all(order, inverse_ref, log_ref, *scratch)


def packed_inverse_kernel(info_ref, both_ref, inverse_ref, log_ref, own_ref, *scratch):
    order, half = own_ref.shape
    places = (((0, 0), (1, 0), (2, 0), (1, 1), (2, 1)), ((0, 3), (1, 3), (2, 3), (3, 3), (2, 2)))
    for source in range(2):
        for k, (row, column) in enumerate(places[source]):
            value = both_ref[source, k * BLOCK : (k + 1) * BLOCK, :]
            rows = slice(row * BLOCK, (row + 1) * BLOCK)
            columns = slice(column * BLOCK, (column + 1) * BLOCK)
            inverse_ref[rows, columns] = value
            if row != column:
                inverse_ref[columns, rows] = value.T
    own = pl.ds(pl.multiple_of(info_ref[0] * half, half), half)
    own_ref[...] = inverse_ref[:, own]
    eliminate_all(order, inverse_ref, log_ref, *scratch)


def inverse_scratch(order):
    return [
        pltpu.VMEM((order, 3 * TILE), BF16),
        pltpu.VMEM((3 * TILE, order), BF16),
        pltpu.VMEM((TILE, TILE), F32),
        pltpu.VMEM((TILE, TILE), F32),
    ]


def inverse_and_log(matrix):
    order = matrix.shape[0]
    return local_call(
        inverse_kernel, "first_inverse", 24 * order**3, 16,
        out_shape=[shape_of(order, order), shape_of(8, TILE)],
        in_specs=vmem(1), out_specs=vmem(2), scratch_shapes=inverse_scratch(order),
    )(matrix)


def inverse_of_packed(info, both, order, half):
    return local_call(
        packed_inverse_kernel, "second_inverse", 24 * order**3, 20,
        out_shape=[shape_of(order, order), shape_of(8, TILE), shape_of(order, half)],
        in_specs=[SMEM_SPEC, *vmem(1)], out_specs=vmem(3), scratch_shapes=inverse_scratch(order),
    )(info, both)


def times(left, right, left_dim=1, right_dim=0):
    dims = (((left_dim,), (right_dim,)), ((), ()))

    def dot(a, b):
        return lax.dot_general(a, b, dims, preferred_element_type=F32)

    return dot(left[0], right[0]) + (dot(left[0], right[1]) + dot(left[1], right[0]))


def split_rows(source, high_ref, low_ref, sign=1):
    def part(r, carry):
        high, low = split_two(sign * source[tile_span(r), :])
        high_ref[tile_span(r), :] = high
        low_ref[tile_span(r), :] = low
        return carry

    lax.fori_loop(0, high_ref.shape[0] // TILE, part, 0)


def block_span(index):
    return pl.ds(pl.multiple_of(index * BLOCK, BLOCK), BLOCK)


def packed_place(core, k):
    row = jnp.where(core == 0, jnp.where(k < 3, k, k - 2), jnp.where(k < 4, k, 2))
    column = jnp.where(core == 0, jnp.where(k < 3, 0, 1), jnp.where(k < 4, 1, 0))
    return row, column


def solve_into(inverse, right, out, right_dim):
    def part(r, carry):
        rows = block_span(r)
        value = times((inverse[0][rows, :], inverse[1][rows, :]), right, 1, right_dim)
        out[0][rows, :], out[1][rows, :] = split_two(value)
        return carry

    lax.fori_loop(0, inverse[0].shape[0] // BLOCK, part, 0)


def packed_gram(core, former, solved, left_dim, store):
    def part(k, carry):
        row, column = packed_place(core, k)
        if left_dim == 0:
            left = (former[0][:, block_span(row)], former[1][:, block_span(row)])
        else:
            left = (former[0][block_span(row), :], former[1][block_span(row), :])
        right = (solved[0][:, block_span(column)], solved[1][:, block_span(column)])
        store(k, row, column, times(left, right, left_dim, 0))
        return carry

    lax.fori_loop(0, PACKED, part, 0)


def arrow_pack(value):
    return jnp.concatenate([value[:, :BLOCK], value[:, BLOCK:]], axis=0)


def arrow_unpack(value):
    effects = value.shape[0] // 2
    return jnp.concatenate([value[:effects], value[effects:]], axis=1)


def first_products_kernel(
    info_ref, inverse_ref, sub_ref, arrow_ref, diag_ref, own_arrow_ref,
    swap_ref, lower_ref, upper_ref, xh_ref, xl_ref,
    vh, vl, bh, bl, sh, sl, yh, yl,
):
    core, even = info_ref[0], info_ref[1] == 1
    half = diag_ref.shape[2]
    own = pl.ds(pl.multiple_of(core * half, half), half)
    split_rows(inverse_ref, vh, vl, -1)
    split_rows(sub_ref.at[0], bh, bl)
    split_rows(sub_ref.at[1], sh, sl)
    solve_into((vh, vl), (bh[:, own], bl[:, own]), (xh_ref, xl_ref), 0)
    solve_into((vh, vl), (sh[own, :], sl[own, :]), (yh, yl), 1)

    def store_lower(k, row, column, value):
        lower_ref[block_span(k), :] = value

    def store_upper(k, row, column, value):
        value = diag_ref[0, block_span(row), block_span(column)] - value
        upper_ref[block_span(k), :] = value
        swap_ref[block_span(k), :] = jnp.where(even, value, lower_ref[block_span(k), :])

    packed_gram(core, (bh, bl), (xh_ref, xl_ref), 0, store_lower)
    packed_gram(core, (sh, sl), (yh, yl), 1, store_upper)
    rows = split_two(arrow_ref[0])
    lower_arrow = arrow_pack(times(rows, (xh_ref[...], xl_ref[...])))
    upper_arrow = arrow_pack(own_arrow_ref[0] - times(rows, (yh[...], yl[...])))
    last = slice(PACKED * BLOCK, None)
    lower_ref[last, :] = lower_arrow
    upper_ref[last, :] = upper_arrow
    swap_ref[last, :] = jnp.where(even, upper_arrow, lower_arrow)


def arrow_form(rows, inverse_ref):
    pieces = split_two(rows)
    through = -times(pieces, split_two(inverse_ref[...]))
    return times(split_two(through), pieces, 1, 1)


def first_fill_kernel(info_ref, inverse_ref, sub_ref, arrow_ref, xh_ref, xl_ref, left_ref, tip_ref, sh, sl):
    keep = info_ref[2] == 1
    split_rows(sub_ref.at[0], sh, sl)

    def part(r, carry):
        rows = block_span(r)
        value = -times((sh[rows, :], sl[rows, :]), (xh_ref[...], xl_ref[...]))
        left_ref[rows, :] = jnp.where(keep, value, 0.0)
        return carry

    lax.fori_loop(0, sh.shape[0] // BLOCK, part, 0)
    tip_ref[...] = arrow_form(arrow_ref[0], inverse_ref)


def separator_arrow(sep_ref):
    last = slice(PACKED * BLOCK, None)
    return jnp.concatenate([arrow_unpack(sep_ref[0, last, :]), arrow_unpack(sep_ref[1, last, :])], axis=1)


def second_products_kernel(
    info_ref, inverse_ref, left_ref, sep_ref, upper_ref, above_ref, out_ref, vh, vl, bh, bl, xh, xl
):
    core, even = info_ref[0], info_ref[1] == 1
    half = xh.shape[1]
    own = pl.ds(pl.multiple_of(core * half, half), half)
    split_rows(inverse_ref, vh, vl, -1)
    split_rows(left_ref, bh, bl)
    rows = split_two(separator_arrow(sep_ref))
    last = slice(PACKED * BLOCK, None)

    @pl.when(even)
    def _():
        solve_into((vh, vl), (bh[:, own], bl[:, own]), (xh, xl), 0)

        def store(k, row, column, value):
            out_ref[block_span(k), :] = value

        packed_gram(core, (bh, bl), (xh, xl), 0, store)
        out_ref[last, :] = arrow_pack(times(rows, (xh[...], xl[...])))

    @pl.when(jnp.logical_not(even))
    def _():
        solve_into((vh, vl), (bh[own, :], bl[own, :]), (xh, xl), 1)

        def store(k, row, column, value):
            span = block_span(k)
            out_ref[span, :] = upper_ref[span, :] - above_ref[span, :] - value

        packed_gram(core, (bh, bl), (xh, xl), 1, store)
        change = arrow_pack(times(rows, (xh[...], xl[...])))
        out_ref[last, :] = upper_ref[last, :] - above_ref[last, :] - change


def second_fill_kernel(
    info_ref, inverse_ref, left_ref, sep_ref, own_ref, pair_ref, tip_ref, log_ref, log_two_ref,
    out_ref, sums_ref, vh, vl, bh, bl, xh, xl,
):
    even = info_ref[1] == 1
    effects = tip_ref.shape[0]
    sums_ref[...] = jnp.zeros_like(sums_ref)

    @pl.when(even)
    def _():
        out_ref[0] = own_ref[...]
        tip = tip_ref[...] + arrow_form(separator_arrow(sep_ref), inverse_ref)
        sums_ref[0:effects, 0:effects] = tip
        sums_ref[effects:, :] = log_ref[...] + log_two_ref[...]

    @pl.when(jnp.logical_not(even))
    def _():
        sums_ref[0:effects, 0:effects] = tip_ref[...]
        sums_ref[effects:, :] = log_ref[...]
        split_rows(inverse_ref, vh, vl, -1)
        split_rows(left_ref, bh, bl)
        solve_into((vh, vl), split_two(pair_ref[...]), (xh, xl), 0)

        def part(r, carry):
            rows = block_span(r)
            out_ref[0, rows, :] = -times((bh[rows, :], bl[rows, :]), (xh[...], xl[...]))
            return carry

        lax.fori_loop(0, bh.shape[0] // BLOCK, part, 0)


def meet(devices):
    barrier = pltpu.get_barrier_semaphore()
    for device in devices:
        pl.semaphore_signal(barrier, inc=1, device_id=device, device_id_type=pl.DeviceIdType.MESH)
    pl.semaphore_wait(barrier, len(devices))


def gather_kernel(diag_ref, out_ref, local_sem, send_sem, recv_sem):
    core = lax.axis_index("blk")
    peer = {"blk": 1 - core}
    half = diag_ref.shape[2]
    rows = diag_ref.shape[1] // COPIES
    own = pl.ds(pl.multiple_of(core * half, half), half)
    local = pltpu.make_async_copy(diag_ref.at[0], out_ref.at[:, own], local_sem)
    local.start()
    meet([peer])
    copies = []
    for k in range(COPIES):
        span = pl.ds(k * rows, rows)
        copies.append(
            pltpu.make_async_remote_copy(
                src_ref=diag_ref.at[0, span, :],
                dst_ref=out_ref.at[span, own],
                send_sem=send_sem.at[k],
                recv_sem=recv_sem.at[k],
                device_id=peer,
                device_id_type=pl.DeviceIdType.MESH,
            )
        )
        copies[-1].start()
    local.wait()
    for copy in copies:
        copy.wait()


def combine_kernel(other_ref, upper_ref, lower_ref, out_ref, sum_ref, local_sem, send_sem, recv_sem):
    core = lax.axis_index("blk")
    even = lax.axis_index("tm") % 2 == 0
    peer = {"blk": 1 - core}
    other = other_ref[...]
    sum_ref[...] = jnp.where(even, upper_ref[...] - other, other - lower_ref[...])
    local = pltpu.make_async_copy(sum_ref, out_ref.at[core], local_sem)
    local.start()
    meet([peer])
    copies = []
    rows = sum_ref.shape[0] // COPIES
    for k in range(COPIES):
        span = pl.ds(k * rows, rows)
        copies.append(
            pltpu.make_async_remote_copy(
                src_ref=sum_ref.at[span, :],
                dst_ref=out_ref.at[core, span, :],
                send_sem=send_sem.at[k],
                recv_sem=recv_sem.at[k],
                device_id=peer,
                device_id_type=pl.DeviceIdType.MESH,
            )
        )
        copies[-1].start()
    local.wait()
    for copy in copies:
        copy.wait()


def finish_kernel(kept_ref, above_ref, out_ref, peer_ref, send_sem, recv_sem):
    core = lax.axis_index("blk")
    peer = {"blk": 1 - core}
    out_ref[...] = kept_ref[...] - above_ref[...]
    meet([peer])
    copies = []
    for slot, block in enumerate((2 - 2 * core, 4 - 3 * core)):
        copies.append(
            pltpu.make_async_remote_copy(
                src_ref=out_ref.at[block_span(block), :],
                dst_ref=peer_ref.at[pl.ds(slot * BLOCK, BLOCK), :],
                send_sem=send_sem.at[slot],
                recv_sem=recv_sem.at[slot],
                device_id=peer,
                device_id_type=pl.DeviceIdType.MESH,
            )
        )
        copies[-1].start()
    for copy in copies:
        copy.wait()


def place_kernel(info_ref, packed_ref, peer_ref, separator_ref, out_ref):
    core, even = info_ref[0], info_ref[1] == 1

    @pl.when(even)
    def _():
        out_ref[0] = separator_ref[...]

    def packed(k):
        return packed_ref[k * BLOCK : (k + 1) * BLOCK, :]

    def put(row, column, value):
        out_ref[0, row * BLOCK : (row + 1) * BLOCK, column * BLOCK : (column + 1) * BLOCK] = value

    first, second = peer_ref[:BLOCK, :], peer_ref[BLOCK:, :]
    odd = jnp.logical_not(even)

    @pl.when(odd & (core == 0))
    def _():
        for row, column, value in (
            (0, 0, packed(0)), (1, 0, packed(1)), (2, 0, packed(2)), (3, 0, first.T),
            (0, 1, packed(1).T), (1, 1, packed(3)), (2, 1, packed(4)), (3, 1, second.T),
        ):
            put(row, column, value)

    @pl.when(odd & (core == 1))
    def _():
        for row, column, value in (
            (0, 0, first.T), (1, 0, second.T), (2, 0, packed(4)), (3, 0, packed(2).T),
            (0, 1, packed(0)), (1, 1, packed(1)), (2, 1, packed(2)), (3, 1, packed(3)),
        ):
            put(row, column, value)


def reduce_kernel(sides, value_ref, out_ref, parts_ref, send_sem, recv_sem):
    me = lax.axis_index("tm")
    stages = []
    stride = 1
    for side in reversed(sides):
        place = (me // stride) % side
        stages.append((side, place, stride))
        stride = stride * side

    def other(stage, step):
        side, place, stride = stages[stage]
        return me + ((place + step) % side - place) * stride

    meet([{"tm": other(s, d)} for s in range(len(stages)) for d in range(1, stages[s][0])])
    out_ref[...] = value_ref[...]
    for s, (side, place, _) in enumerate(stages):
        parts_ref[s, place] = out_ref[...]
        copies = []
        for d in range(1, side):
            copies.append(
                pltpu.make_async_remote_copy(
                    src_ref=out_ref,
                    dst_ref=parts_ref.at[s, place],
                    send_sem=send_sem.at[s, d],
                    recv_sem=recv_sem.at[s, d],
                    device_id={"tm": other(s, d)},
                    device_id_type=pl.DeviceIdType.MESH,
                )
            )
            copies[-1].start()
        for copy in copies:
            copy.wait()
        total = parts_ref[s, 0]
        for k in range(1, side):
            total = total + parts_ref[s, k]
        out_ref[...] = total


def vmem(count):
    return [pl.BlockSpec(memory_space=pltpu.VMEM)] * count


def shape_of(*sizes, dtype=F32):
    return jax.ShapeDtypeStruct(sizes, dtype)


SMEM_SPEC = pl.BlockSpec(memory_space=pltpu.SMEM)
ANY_SPEC = pl.BlockSpec(memory_space=pl.ANY)


def local_call(kernel, name, flops, mebibytes, **kwargs):
    return pl.pallas_call(
        kernel,
        compiler_params=pltpu.CompilerParams(vmem_limit_bytes=mebibytes * 2**20),
        cost_estimate=pl.CostEstimate(flops=flops, bytes_accessed=2**23, transcendentals=0),
        name=name,
        **kwargs,
    )


def remote_call(kernel, name, identity, **kwargs):
    return pl.pallas_call(
        kernel,
        compiler_params=pltpu.CompilerParams(
            collective_id=identity, has_side_effects=True, vmem_limit_bytes=24 * 2**20
        ),
        name=name,
        **kwargs,
    )


def dma_sems(*shape):
    return pltpu.SemaphoreType.DMA(shape)


def whole(shape, index):
    return pl.BlockSpec(shape, lambda i: index, pipeline_mode=pl.Buffered(1))


def on_device(diag_blocks, sub_blocks, arrow_blocks, tip_block):
    partition = lax.axis_index("tm")
    parts = lax.axis_size("tm")
    order, half = diag_blocks.shape[1:]
    effects = arrow_blocks.shape[1]
    packed_rows = PACKED * BLOCK + effects * half // BLOCK
    evens = range(0, parts, 2)
    down = [(p, p - 1) for p in evens if p > 0]
    core = lax.axis_index("blk")
    info = jnp.stack([core, (partition % 2 == 0).astype(core.dtype), (partition > 0).astype(core.dtype)])
    square, tall = (order, order), (order, half)
    big = [pltpu.VMEM(square, BF16)] * 2
    thin = [pltpu.VMEM(tall, BF16)] * 2

    pivot = remote_call(
        gather_kernel, "gather_pivot", 1,
        out_shape=shape_of(*square), in_specs=[ANY_SPEC], out_specs=ANY_SPEC,
        scratch_shapes=[pltpu.SemaphoreType.DMA, dma_sems(COPIES), dma_sems(COPIES)],
    )(diag_blocks)
    sub_full = lax.all_gather(sub_blocks, "blk", axis=2, tiled=True)
    arrow_full = lax.all_gather(arrow_blocks, "blk", axis=2, tiled=True)
    inverse, log_first = inverse_and_log(pivot)

    packed_shape = shape_of(packed_rows, BLOCK)
    swap, lower, upper, x_high, x_low = local_call(
        first_products_kernel, "first_products", 10 * order**3, 44,
        grid=(1,),
        out_shape=[packed_shape] * 3 + [shape_of(*tall, dtype=BF16)] * 2,
        in_specs=[SMEM_SPEC, *vmem(3), whole((1, *tall), (1, 0, 0)), whole((1, effects, half), (1, 0, 0))],
        out_specs=vmem(5),
        scratch_shapes=big * 3 + thin,
    )(info, inverse, sub_full, arrow_full, diag_blocks, arrow_blocks)
    pairs = [(p, p + 1) for p in evens]
    other = lax.ppermute(swap, "tm", pairs + [(b, a) for a, b in pairs])
    left_own, tip_first = local_call(
        first_fill_kernel, "first_fill", 3 * order**3, 32,
        grid=(1,),
        out_shape=[shape_of(*tall), shape_of(effects, effects)],
        in_specs=[SMEM_SPEC, *vmem(1), whole((1, *square), (1, 0, 0)), whole((1, effects, order), (0, 0, 0)), *vmem(2)],
        out_specs=vmem(2),
        scratch_shapes=big,
    )(info, inverse, sub_full, arrow_full, x_high, x_low)
    lower_above = lax.ppermute(lower, "tm", down)
    left_pair = lax.ppermute(left_own, "tm", pairs)
    left_full = lax.all_gather(left_own, "blk", axis=1, tiled=True)

    both = remote_call(
        combine_kernel, "gather_separator", 2,
        out_shape=shape_of(2, packed_rows, BLOCK), in_specs=vmem(3), out_specs=ANY_SPEC,
        scratch_shapes=[
            pltpu.VMEM((packed_rows, BLOCK), F32),
            pltpu.SemaphoreType.DMA, dma_sems(COPIES), dma_sems(COPIES),
        ],
    )(other, upper, lower)
    inverse, log_second, separator = inverse_of_packed(info, both, order, half)
    product = local_call(
        second_products_kernel, "second_products", 5 * order**3, 40,
        out_shape=packed_shape,
        in_specs=[SMEM_SPEC, *vmem(5)],
        out_specs=vmem(1)[0],
        scratch_shapes=big * 2 + thin,
    )(info, inverse, left_full, both, upper, lower_above)
    above = lax.ppermute(product, "tm", down)
    left_result, sums = local_call(
        second_fill_kernel, "second_fill", 6 * order**3, 44,
        out_shape=[shape_of(1, *tall), shape_of(effects + 8, TILE)],
        in_specs=[SMEM_SPEC, *vmem(8)],
        out_specs=vmem(2),
        scratch_shapes=big * 2 + thin,
    )(info, inverse, left_full, both, left_own, left_pair, tip_first, log_first, log_second)
    sides = side_lengths(parts)
    totals = remote_call(
        functools.partial(reduce_kernel, sides), "reduce_terms", 3,
        out_shape=shape_of(effects + 8, TILE), in_specs=vmem(1), out_specs=vmem(1)[0],
        scratch_shapes=[
            pltpu.VMEM((len(sides), max(sides), effects + 8, TILE), F32),
            dma_sems(len(sides), max(sides)), dma_sems(len(sides), max(sides)),
        ],
    )(sums)
    packed, swapped = remote_call(
        finish_kernel, "finish_blocks", 4,
        out_shape=[packed_shape, shape_of(2 * BLOCK, BLOCK)], in_specs=vmem(2), out_specs=vmem(2),
        scratch_shapes=[dma_sems(2), dma_sems(2)],
    )(product, above)
    diag_result = local_call(
        place_kernel, "place_blocks", 2**20, 12,
        out_shape=shape_of(1, *tall), in_specs=[SMEM_SPEC, *vmem(3)], out_specs=vmem(1)[0],
    )(info, packed, swapped, separator)
    last = PACKED * BLOCK
    own_arrow = lax.dynamic_index_in_dim(both[:, last:], core, 0, keepdims=False)
    arrow_result = arrow_unpack(jnp.where(info[1] == 1, own_arrow, packed[last:]))
    return (
        diag_result,
        left_result,
        arrow_result[None],
        tip_block - totals[:effects, :effects],
        jnp.sum(totals[effects]),
    )


def side_lengths(parts):
    sides = []
    while parts > 1:
        side = 4 if parts % 4 == 0 else parts
        sides.append(side)
        parts //= side
    return tuple(sides)


def solution(mesh):
    in_specs = (P("tm", None, "blk"), P("tm", None, "blk"), P("tm", None, "blk"), P())
    out_specs = (P("tm", None, "blk"), P("tm", None, "blk"), P("tm", None, "blk"), P(), P())
    return jax.shard_map(
        on_device, mesh=mesh, in_specs=in_specs, out_specs=out_specs, check_vma=False
    )
```

profile of v0, /device:TPU:25, one launch (start us, length us, event | category | flops | bytes accessed | tf_op | source)
XLA Modules:
  0.0 252.3 jit_solution(7185963919857119294)
XLA Ops:
  8.0 2.2 copy-done.2
  10.2 4.9 %gather_pivot.1.source_ref = f32[1024,1024]{1,0:T(8,128)S(1)} custom-call(f32[2,1024,512]{2,1,0:T(8,128)S(1)} %copy-done.2), custom_call_target="tpu_custom_call" | custom-call | tf_op jit(solution)/shard_map/gather_pivot/pallas_call | solution.py:624
  15.2 2.2 all_gather.10.arrow_ref
  17.4 33.8 %first_inverse.1 = (f32[1024,1024]{1,0:T(8,128)S(1)}, f32[8,128]{1,0:T(8,128)S(1)}) custom-call(f32[1024,1024]{1,0:T(8,128)S(1)} %gather_pivot.1.source_ref), custom_call_target="tpu_custom_call" | custom-call | flops 25769803776 | bytes 8388608 | tf_op jit(solution)/shard_map/first_inverse/pallas_call | solution.py:212
  51.1 2.0 copy-done
  53.1 24.4 %first_products.1 = (f32[1408,256]{1,0:T(8,128)S(1)}, f32[1408,256]{1,0:T(8,128)}, f32[1408,256]{1,0:T(8,128)S(1)}, bf16[1024,512]{1,0:T(8,128)(2,1)S(1)}, bf16[1024,512]{1,0:T(8,128)(2,1)S(1)}) custom-call(s32[3]{0:T(128)S(1)} %pad_add_fusion.info_ref, f32[1024,1024]{1,0:T(8,128)} %copy-done, f32[2,1024,1024]{2,1,0:T(8,128)} %all-gather.3.cloned.1.call-done.sub_ref, ...), custom_call_target="tpu_custom_call" | custom-call | flops 10737418240 | bytes 8388608 | tf_op jit(solution)/shard_map/first_products/pallas_call | solution.py:634
  78.6 7.6 %first_fill.1 = (f32[1024,512]{1,0:T(8,128)}, f32[64,64]{1,0:T(8,128)S(1)}) custom-call(s32[3]{0:T(128)S(1)} %pad_add_fusion.info_ref, f32[1024,1024]{1,0:T(8,128)S(1)} %copy-done.1, f32[2,1024,1024]{2,1,0:T(8,128)S(1)} %bitcast.8, f32[2,64,1024]{2,1,0:T(8,128)S(1)} %all_gather.10.arrow_ref, bf16[1024,512]{1,0:T(8,128)(2,1)S(1)} %get-tuple-element.26.xh_ref, ...), custom_call_target="tpu_custom_call" | custom-call | flops 3221225472 | bytes 8388608 | tf_op jit(solution)/shard_map/first_fill/pallas_call | solution.py:644
  86.2 1.3 copy-done.11
  88.0 1.3 collective-permute-start.3
  89.3 1.5 collective-permute-start.1
  90.8 29.6 %collective-permute-done.other_ref = f32[1408,256]{1,0:T(8,128)S(1)} collective-permute-done((f32[1408,256]{1,0:T(8,128)S(1)}, f32[1408,256]{1,0:T(8,128)S(1)}, u32[]{:S(2)}, u32[]{:S(2)}) %collective-permute-start) | collective-permute-done | bytes 1441824 | tf_op jit(solution)/shard_map/ppermute | solution.py:643
  120.4 1.4 copy-done.7
  121.7 6.8 %gather_separator.1.both_ref.sep_ref = f32[2,1408,256]{2,1,0:T(8,128)S(1)} custom-call(f32[1408,256]{1,0:T(8,128)S(1)} %collective-permute-done.other_ref, f32[1408,256]{1,0:T(8,128)S(1)} %copy-done.7, f32[1408,256]{1,0:T(8,128)} %get-tuple-element.24.lower_ref), custom_call_target="tpu_custom_call" | custom-call | tf_op jit(solution)/shard_map/gather_separator/pallas_call | solution.py:656
  128.5 34.6 %second_inverse.1 = (f32[1024,1024]{1,0:T(8,128)S(1)}, f32[8,128]{1,0:T(8,128)S(1)}, f32[1024,512]{1,0:T(8,128)S(1)}) custom-call(s32[3]{0:T(128)S(1)} %pad_add_fusion.info_ref, f32[2,1408,256]{2,1,0:T(8,128)S(1)} %gather_separator.1.both_ref.sep_ref), custom_call_target="tpu_custom_call" | custom-call | flops 25769803776 | bytes 8388608 | tf_op jit(solution)/shard_map/second_inverse/pallas_call | solution.py:220
  163.1 1.4 copy-done.4
  164.6 2.0 copy-done.14
  167.7 1.4 copy-done.8
  169.1 1.4 copy-done.13
  170.4 2.2 copy-done.15
  172.6 12.8 %second_products.1.kept_ref = f32[1408,256]{1,0:T(8,128)} custom-call(s32[3]{0:T(128)S(1)} %pad_add_fusion.info_ref, f32[1024,1024]{1,0:T(8,128)S(1)} %copy-done.15, f32[1024,1024]{1,0:T(8,128)} %all-gather.5.cloned.1.call-done.left_ref, f32[2,1408,256]{2,1,0:T(8,128)S(1)} %gather_separator.1.both_ref.sep_ref, f32[1408,256]{1,0:T(8,128)S(1)} %copy-done.8, ...), custom_call_target="tpu_custom_call" | custom-call | flops 5368709120 | bytes 8388608 | tf_op jit(solution)/shard_map/second_products/pallas_call | solution.py:665
  186.8 16.2 %second_fill.1 = (f32[1,1024,512]{2,1,0:T(8,128)}, f32[72,128]{1,0:T(8,128)S(1)}) custom-call(s32[3]{0:T(128)S(1)} %pad_add_fusion.info_ref, f32[1024,1024]{1,0:T(8,128)} %copy-done.14, f32[1024,1024]{1,0:T(8,128)} %all-gather.5.cloned.1.call-done.left_ref, f32[2,1408,256]{2,1,0:T(8,128)S(1)} %gather_separator.1.both_ref.sep_ref, ...), custom_call_target="tpu_custom_call" | custom-call | flops 6442450944 | bytes 8388608 | tf_op jit(solution)/shard_map/second_fill/pallas_call | solution.py:673
  202.9 33.1 %reduce_terms.1 = f32[72,128]{1,0:T(8,128)S(1)} custom-call(f32[72,128]{1,0:T(8,128)S(1)} %get-tuple-element.36.value_ref), custom_call_target="tpu_custom_call" | custom-call | tf_op jit(solution)/shard_map/reduce_terms/pallas_call | solution.py:681
  237.2 5.3 %finish_blocks.1 = (f32[1408,256]{1,0:T(8,128)S(1)}, f32[512,256]{1,0:T(8,128)S(1)}) custom-call(f32[1408,256]{1,0:T(8,128)} %second_products.1.kept_ref, f32[1408,256]{1,0:T(8,128)} %collective-permute-done.2.above_ref), custom_call_target="tpu_custom_call" | custom-call | tf_op jit(solution)/shard_map/finish_blocks/pallas_call | solution.py:689
  243.3 2.2 place_blocks.1
  (49 shorter events, 6.8 us)
Async XLA Ops:
  7.2 46.0 %all-gather.3.cloned.1.call-start = ((), (), s32[]{:S(2)}) async-start(), calls=%async_computation | async-start | bytes 12582912 | tf_op jit(solution)/shard_map/all_gather | solution.py:629
  7.9 159.8 %all-gather.5.cloned.1.call-start = ((), (), s32[]{:S(2)}) async-start(), calls=%async_computation.1 | async-start | bytes 6291456 | tf_op jit(solution)/shard_map/all_gather | solution.py:654
  8.0 2.2 copy-start.2
  10.2 5.0 %copy-start.9 = (f32[2,64,512]{2,1,0:T(8,128)S(1)}, f32[2,64,512]{2,1,0:T(8,128)}, u32[]{:S(2)}) copy-start(f32[2,64,512]{2,1,0:T(8,128)} %own_arrow_ref.1) | copy-start | bytes 786436
  51.1 2.0 copy-start
  53.1 25.5 %slice-start = ((s8[8388608]{0:T(1024)(128)(4,1)}), s8[4194304]{0:T(1024)(128)(4,1)S(1)}, s32[]{:S(2)}) async-start(s8[8388608]{0:T(1024)(128)(4,1)} %bitcast.7), calls=%async_computation.2 | async-start | bytes 8388608
  53.1 25.5 %slice-start.1 = ((s8[8388608]{0:T(1024)(128)(4,1)}), s8[4194304]{0:T(1024)(128)(4,1)S(1)}, s32[]{:S(2)}) async-start(s8[8388608]{0:T(1024)(128)(4,1)} %bitcast.7), calls=%async_computation.3 | async-start | bytes 8388608
  53.1 25.5 %copy-start.1 = (f32[1024,1024]{1,0:T(8,128)S(1)}, f32[1024,1024]{1,0:T(8,128)}, u32[]{:S(2)}) copy-start(f32[1024,1024]{1,0:T(8,128)} %copy-done) | copy-start | bytes 12582916
  78.6 7.6 %copy-start.10 = (f32[1408,256]{1,0:T(8,128)}, f32[1408,256]{1,0:T(8,128)S(1)}, u32[]{:S(2)}) copy-start(f32[1408,256]{1,0:T(8,128)S(1)} %get-tuple-element.22) | copy-start | bytes 4325380
  86.2 1.4 copy-start.11
  87.6 32.8 %collective-permute-start = (f32[1408,256]{1,0:T(8,128)S(1)}, f32[1408,256]{1,0:T(8,128)S(1)}, u32[]{:S(2)}, u32[]{:S(2)}) collective-permute-start(f32[1408,256]{1,0:T(8,128)S(1)} %copy-done.11), channel_id=1, source_target_pairs={{0,2},{4,6},{8,10},{12,14},{16,18},{20,22},{24,26},{28,30},{32,34}... | collective-permute-start | bytes 4325384 | tf_op jit(solution)/shard_map/ppermute | solution.py:643
  88.0 98.7 %collective-permute-start.3 = (f32[1024,512]{1,0:T(8,128)}, f32[1024,512]{1,0:T(8,128)}, u32[]{:S(2)}, u32[]{:S(2)}) collective-permute-start(f32[1024,512]{1,0:T(8,128)} %get-tuple-element.28.own_ref), channel_id=1, source_target_pairs={{0,2},{4,6},{8,10},{12,14},{16,18},{20,22},{24,26},{28,30},{32,34}... | collective-permute-start | bytes 6291464 | tf_op jit(solution)/shard_map/ppermute | solution.py:653
  89.3 77.3 %collective-permute-start.1 = (f32[1408,256]{1,0:T(8,128)}, f32[1408,256]{1,0:T(8,128)S(1)}, u32[]{:S(2)}, u32[]{:S(2)}) collective-permute-start(f32[1408,256]{1,0:T(8,128)} %get-tuple-element.24.lower_ref), channel_id=1, source_target_pairs={{4,2},{8,6},{12,10},{16,14},{20,18},{24,22},{28,26},{32,30},{36,34... | collective-permute-start | bytes 4325384 | tf_op jit(solution)/shard_map/ppermute | solution.py:652
  120.4 1.4 copy-start.7
  128.5 58.2 %copy-start.3 = (f32[2,1408,256]{2,1,0:T(8,128)}, f32[2,1408,256]{2,1,0:T(8,128)S(1)}, u32[]{:S(2)}) copy-start(f32[2,1408,256]{2,1,0:T(8,128)S(1)} %gather_separator.1.both_ref.sep_ref) | copy-start | bytes 8650756
  163.1 1.5 copy-start.4
  164.6 2.0 copy-start.14
  167.7 1.4 copy-start.8
  169.1 1.4 copy-start.13
  170.4 2.2 copy-start.15
  185.4 51.8 %collective-permute-start.2 = (f32[1408,256]{1,0:T(8,128)}, f32[1408,256]{1,0:T(8,128)}, u32[]{:S(2)}, u32[]{:S(2)}) collective-permute-start(f32[1408,256]{1,0:T(8,128)} %second_products.1.kept_ref), channel_id=1, source_target_pairs={{4,2},{8,6},{12,10},{16,14},{20,18},{24,22},{28,26},{32,30},{36,34... | collective-permute-start | bytes 4325384 | tf_op jit(solution)/shard_map/ppermute | solution.py:672
  186.7 49.9 %copy-start.16 = (f32[64,64]{1,0:T(8,128)S(1)}, f32[64,64]{1,0:T(8,128)}, u32[]{:S(2)}) copy-start(f32[64,64]{1,0:T(8,128)} %param.7) | copy-start | bytes 49156
  202.9 39.6 %slice-start.2 = ((f32[2,1408,256]{2,1,0:T(8,128)}), f32[2,128,256]{2,1,0:T(8,128)S(1)}, s32[]{:S(2)}) async-start(f32[2,1408,256]{2,1,0:T(8,128)} %copy-done.3), calls=%async_computation.4 | async-start | bytes 524288 | tf_op jit(solution)/shard_map/slice | solution.py:699
  202.9 40.4 %copy-start.5 = (f32[1024,512]{1,0:T(8,128)S(1)}, f32[1024,512]{1,0:T(8,128)}, u32[]{:S(2)}) copy-start(f32[1024,512]{1,0:T(8,128)} %copy-done.4) | copy-start | bytes 6291460
  (2 other events, 2.2 us)
Sparse Core Ops, SparseCore 0:
  9.7 25.1 all-gather.2
  86.4 18.7 all-gather.4
where the time goes:
time: 253 us; the launch traced here: 252 us
  Pallas kernels  182 us (72%)
  waiting for transfers between devices  30.3 us (12%)
  local copies, waits for them, and re-layouts  17.5 us (7%)
  between operations  14.2 us (6%)
  starting transfers between devices  4.57 us (2%)
    pallas_call x1, Pallas kernels, inverse_of_packed(): local_call(packed_inverse_kernel, 'second_inverse', 24 * order ** 3, 20,...  34.6 us
    pallas_call x1, Pallas kernels, inverse_and_log(): local_call(inverse_kernel, 'first_inverse', 24 * order ** 3, 16, out_shap...  33.8 us
    pallas_call x1, Pallas kernels, on_device(): remote_call(functools.partial(reduce_kernel, sides), 'reduce_terms', 3, o...  33.1 us
    ppermute x1, waiting for transfers between devices, on_device(): other = lax.ppermute(swap, 'tm', pairs + [(b, a) for a, b in pairs])  29.6 us
    pallas_call x1, Pallas kernels, on_device(): local_call(first_products_kernel, 'first_products', 10 * order ** 3, 44,...  24.4 us
    unnamed x38, local copies, waits for them, and re-layouts  17.5 us
    pallas_call x1, Pallas kernels, on_device(): local_call(second_fill_kernel, 'second_fill', 6 * order ** 3, 44, out_sha...  16.2 us
    pallas_call x1, Pallas kernels, on_device(): local_call(second_products_kernel, 'second_products', 5 * order ** 3, 40,...  12.8 us
  transfers between devices with their start and end apart: 6, of which 1 were waited for; matrix products, arithmetic and copies ran while one was open for 1% of the time, Pallas kernels for 56%

commit v1 on v0

--- a/solution.py
+++ b/solution.py
@@ -286,37 +286,61 @@
     return jnp.concatenate([value[:effects], value[effects:]], axis=1)
 
 
+def fetch(pairs, sems):
+    copies = [pltpu.make_async_copy(source, target, sems.at[k]) for k, (source, target) in enumerate(pairs)]
+    for copy in copies:
+        copy.start()
+    return copies
+
+
 def first_products_kernel(
-    info_ref, inverse_ref, sub_ref, arrow_ref, diag_ref, own_arrow_ref,
-    swap_ref, lower_ref, upper_ref, xh_ref, xl_ref,
-    vh, vl, bh, bl, sh, sl, yh, yl,
+    info_ref, arrow_ref, inverse_hbm, sub_hbm, diag_hbm, own_arrow_hbm,
+    swap_ref, rest_ref, xh_ref, xl_ref,
+    inverse_ref, left_ref, right_ref, diag_ref, own_arrow_ref, sems, vh, vl, bh, bl, sh, sl, yh, yl,
 ):
     core, even = info_ref[0], info_ref[1] == 1
-    half = diag_ref.shape[2]
+    half = diag_ref.shape[1]
     own = pl.ds(pl.multiple_of(core * half, half), half)
+    copies = fetch(
+        (
+            (inverse_hbm, inverse_ref),
+            (sub_hbm.at[0], left_ref),
+            (sub_hbm.at[1], right_ref),
+            (diag_hbm.at[1], diag_ref),
+            (own_arrow_hbm.at[1], own_arrow_ref),
+        ),
+        sems,
+    )
+    copies[0].wait()
     split_rows(inverse_ref, vh, vl, -1)
-    split_rows(sub_ref.at[0], bh, bl)
-    split_rows(sub_ref.at[1], sh, sl)
+    copies[1].wait()
+    split_rows(left_ref, bh, bl)
     solve_into((vh, vl), (bh[:, own], bl[:, own]), (xh_ref, xl_ref), 0)
+    copies[2].wait()
+    split_rows(right_ref, sh, sl)
     solve_into((vh, vl), (sh[own, :], sl[own, :]), (yh, yl), 1)
-
-    def store_lower(k, row, column, value):
-        lower_ref[block_span(k), :] = value
-
-    def store_upper(k, row, column, value):
-        value = diag_ref[0, block_span(row), block_span(column)] - value
-        upper_ref[block_span(k), :] = value
-        swap_ref[block_span(k), :] = jnp.where(even, value, lower_ref[block_span(k), :])
-
-    packed_gram(core, (bh, bl), (xh_ref, xl_ref), 0, store_lower)
-    packed_gram(core, (sh, sl), (yh, yl), 1, store_upper)
+    copies[3].wait()
+    copies[4].wait()
+
+    def keep(span, lower, upper):
+        swap_ref[span, :] = jnp.where(even, upper, lower)
+        rest_ref[span, :] = jnp.where(even, lower, upper)
+
+    def part(k, carry):
+        row, column = packed_place(core, k)
+        rows, columns = block_span(row), block_span(column)
+        lower = times((bh[:, rows], bl[:, rows]), (xh_ref[:, columns], xl_ref[:, columns]), 0, 0)
+        change = times((sh[rows, :], sl[rows, :]), (yh[:, columns], yl[:, columns]))
+        keep(block_span(k), lower, diag_ref[rows, columns] - change)
+        return carry
+
+    lax.fori_loop(0, PACKED, part, 0)
     rows = split_two(arrow_ref[0])
-    lower_arrow = arrow_pack(times(rows, (xh_ref[...], xl_ref[...])))
-    upper_arrow = arrow_pack(own_arrow_ref[0] - times(rows, (yh[...], yl[...])))
-    last = slice(PACKED * BLOCK, None)
-    lower_ref[last, :] = lower_arrow
-    upper_ref[last, :] = upper_arrow
-    swap_ref[last, :] = jnp.where(even, upper_arrow, lower_arrow)
+    keep(
+        slice(PACKED * BLOCK, None),
+        arrow_pack(times(rows, (xh_ref[...], xl_ref[...]))),
+        arrow_pack(own_arrow_ref[...] - times(rows, (yh[...], yl[...]))),
+    )
 
 
 def arrow_form(rows, inverse_ref):
@@ -325,35 +349,35 @@
     return times(split_two(through), pieces, 1, 1)
 
 
-def first_fill_kernel(info_ref, inverse_ref, sub_ref, arrow_ref, xh_ref, xl_ref, left_ref, tip_ref, sh, sl):
-    keep = info_ref[2] == 1
-    split_rows(sub_ref.at[0], sh, sl)
-
-    def part(r, carry):
-        rows = block_span(r)
-        value = -times((sh[rows, :], sl[rows, :]), (xh_ref[...], xl_ref[...]))
-        left_ref[rows, :] = jnp.where(keep, value, 0.0)
-        return carry
-
-    lax.fori_loop(0, sh.shape[0] // BLOCK, part, 0)
-    tip_ref[...] = arrow_form(arrow_ref[0], inverse_ref)
-
-
-def separator_arrow(sep_ref):
-    last = slice(PACKED * BLOCK, None)
-    return jnp.concatenate([arrow_unpack(sep_ref[0, last, :]), arrow_unpack(sep_ref[1, last, :])], axis=1)
+def separator_arrow(packed):
+    return jnp.concatenate([arrow_unpack(packed[0]), arrow_unpack(packed[1])], axis=1)
 
 
 def second_products_kernel(
-    info_ref, inverse_ref, left_ref, sep_ref, upper_ref, above_ref, out_ref, vh, vl, bh, bl, xh, xl
+    info_ref, inverse_hbm, left_hbm, both_hbm, rest_hbm, above_hbm, out_ref,
+    inverse_ref, left_ref, arrow_ref, rest_ref, above_ref, sems, vh, vl, bh, bl, xh, xl,
 ):
     core, even = info_ref[0], info_ref[1] == 1
     half = xh.shape[1]
     own = pl.ds(pl.multiple_of(core * half, half), half)
+    last = slice(PACKED * BLOCK, None)
+    copies = fetch(
+        (
+            (inverse_hbm, inverse_ref),
+            (left_hbm, left_ref),
+            (both_hbm.at[:, pl.ds(PACKED * BLOCK, arrow_ref.shape[1]), :], arrow_ref),
+            (rest_hbm, rest_ref),
+            (above_hbm, above_ref),
+        ),
+        sems,
+    )
+    copies[0].wait()
     split_rows(inverse_ref, vh, vl, -1)
+    copies[1].wait()
     split_rows(left_ref, bh, bl)
-    rows = split_two(separator_arrow(sep_ref))
-    last = slice(PACKED * BLOCK, None)
+    for copy in copies[2:]:
+        copy.wait()
+    rows = split_two(separator_arrow(arrow_ref[...]))
 
     @pl.when(even)
     def _():
@@ -371,11 +395,11 @@
 
         def store(k, row, column, value):
             span = block_span(k)
-            out_ref[span, :] = upper_ref[span, :] - above_ref[span, :] - value
+            out_ref[span, :] = rest_ref[span, :] - above_ref[span, :] - value
 
         packed_gram(core, (bh, bl), (xh, xl), 1, store)
         change = arrow_pack(times(rows, (xh[...], xl[...])))
-        out_ref[last, :] = upper_ref[last, :] - above_ref[last, :] - change
+        out_ref[last, :] = rest_ref[last, :] - above_ref[last, :] - change
 
 
 def second_fill_kernel(
@@ -389,7 +413,7 @@
     @pl.when(even)
     def _():
         out_ref[0] = own_ref[...]
-        tip = tip_ref[...] + arrow_form(separator_arrow(sep_ref), inverse_ref)
+        tip = tip_ref[...] + arrow_form(separator_arrow(sep_ref[:, PACKED * BLOCK :, :]), inverse_ref)
         sums_ref[0:effects, 0:effects] = tip
         sums_ref[effects:, :] = log_ref[...] + log_two_ref[...]
 
@@ -416,22 +440,13 @@
     pl.semaphore_wait(barrier, len(devices))
 
 
-def gather_kernel(diag_ref, out_ref, local_sem, send_sem, recv_sem):
-    core = lax.axis_index("blk")
-    peer = {"blk": 1 - core}
-    half = diag_ref.shape[2]
-    rows = diag_ref.shape[1] // COPIES
-    own = pl.ds(pl.multiple_of(core * half, half), half)
-    local = pltpu.make_async_copy(diag_ref.at[0], out_ref.at[:, own], local_sem)
-    local.start()
-    meet([peer])
+def exchange(parts, peer, send_sem, recv_sem):
     copies = []
-    for k in range(COPIES):
-        span = pl.ds(k * rows, rows)
+    for k, (source, target) in enumerate(parts):
         copies.append(
             pltpu.make_async_remote_copy(
-                src_ref=diag_ref.at[0, span, :],
-                dst_ref=out_ref.at[span, own],
+                src_ref=source,
+                dst_ref=target,
                 send_sem=send_sem.at[k],
                 recv_sem=recv_sem.at[k],
                 device_id=peer,
@@ -439,37 +454,79 @@
             )
         )
         copies[-1].start()
+    return copies
+
+
+def gather_kernel(diag_ref, arrow_ref, out_ref, arrow_out_ref, local_sems, send_sem, recv_sem):
+    core = lax.axis_index("blk")
+    peer = {"blk": 1 - core}
+    half = diag_ref.shape[2]
+    rows = diag_ref.shape[1] // COPIES
+    own = pl.ds(pl.multiple_of(core * half, half), half)
+    local = pltpu.make_async_copy(diag_ref.at[0], out_ref.at[:, own], local_sems.at[0])
+    local.start()
+    local_arrow = pltpu.make_async_copy(arrow_ref.at[0], arrow_out_ref.at[0, :, own], local_sems.at[1])
+    local_arrow.start()
+    meet([peer])
+    spans = [pl.ds(k * rows, rows) for k in range(COPIES)]
+    parts = [(diag_ref.at[0, span, :], out_ref.at[span, own]) for span in spans]
+    parts.append((arrow_ref.at[0], arrow_out_ref.at[0, :, own]))
+    copies = exchange(parts, peer, send_sem, recv_sem)
     local.wait()
+    local_arrow.wait()
     for copy in copies:
         copy.wait()
 
 
-def combine_kernel(other_ref, upper_ref, lower_ref, out_ref, sum_ref, local_sem, send_sem, recv_sem):
-    core = lax.axis_index("blk")
-    even = lax.axis_index("tm") % 2 == 0
-    peer = {"blk": 1 - core}
-    other = other_ref[...]
-    sum_ref[...] = jnp.where(even, upper_ref[...] - other, other - lower_ref[...])
-    local = pltpu.make_async_copy(sum_ref, out_ref.at[core], local_sem)
-    local.start()
-    meet([peer])
-    copies = []
+def pair_kernel(
+    swap_hbm, inverse_hbm, sub_hbm, arrow_hbm, xh_hbm, xl_hbm, both_hbm, left_ref, tip_ref,
+    own_ref, other_ref, sum_ref, inverse_ref, right_ref, arrow_ref, xh, xl, sh, sl,
+    sems, local_sems, swap_send, swap_recv, send_sem, recv_sem,
+):
+    core, me = lax.axis_index("blk"), lax.axis_index("tm")
+    even = me % 2 == 0
+    peer, partner = {"blk": 1 - core}, {"tm": me + 1 - 2 * (me % 2)}
+    meet([peer, partner])
     rows = sum_ref.shape[0] // COPIES
-    for k in range(COPIES):
-        span = pl.ds(k * rows, rows)
-        copies.append(
-            pltpu.make_async_remote_copy(
-                src_ref=sum_ref.at[span, :],
-                dst_ref=out_ref.at[core, span, :],
-                send_sem=send_sem.at[k],
-                recv_sem=recv_sem.at[k],
-                device_id=peer,
-                device_id_type=pl.DeviceIdType.MESH,
-            )
+    spans = [pl.ds(k * rows, rows) for k in range(COPIES)]
+    swaps = exchange(
+        [(swap_hbm.at[span, :], other_ref.at[span, :]) for span in spans], partner, swap_send, swap_recv
+    )
+    copies = fetch(
+        (
+            (sub_hbm.at[1], right_ref),
+            (xh_hbm, xh),
+            (xl_hbm, xl),
+            (inverse_hbm, inverse_ref),
+            (arrow_hbm.at[0], arrow_ref),
+            (swap_hbm, own_ref),
+        ),
+        sems,
+    )
+    for copy in copies:
+        copy.wait()
+    split_rows(right_ref, sh, sl)
+
+    def part(r, carry):
+        span = block_span(r)
+        value = -times((sh[span, :], sl[span, :]), (xh[...], xl[...]))
+        left_ref[span, :] = jnp.where(me > 0, value, 0.0)
+        return carry
+
+    lax.fori_loop(0, sh.shape[0] // BLOCK, part, 0)
+    tip_ref[...] = arrow_form(arrow_ref[...], inverse_ref)
+    shares = []
+    for k, span in enumerate(spans):
+        swaps[k].wait()
+        difference = own_ref[span, :] - other_ref[span, :]
+        sum_ref[span, :] = jnp.where(even, difference, -difference)
+        local = pltpu.make_async_copy(sum_ref.at[span, :], both_hbm.at[core, span, :], local_sems.at[k])
+        local.start()
+        shares.append(local)
+        shares += exchange(
+            [(sum_ref.at[span, :], both_hbm.at[core, span, :])], peer, send_sem.at[pl.ds(k, 1)], recv_sem.at[pl.ds(k, 1)]
         )
-        copies[-1].start()
-    local.wait()
-    for copy in copies:
+    for copy in shares:
         copy.wait()
 
 
@@ -543,7 +600,8 @@
 
     meet([{"tm": other(s, d)} for s in range(len(stages)) for d in range(1, stages[s][0])])
     out_ref[...] = value_ref[...]
-    for s, (side, place, _) in enumerate(stages):
+    for s in reversed(range(len(stages))):
+        side, place, _ = stages[s]
         parts_ref[s, place] = out_ref[...]
         copies = []
         for d in range(1, side):
@@ -576,6 +634,7 @@
 
 SMEM_SPEC = pl.BlockSpec(memory_space=pltpu.SMEM)
 ANY_SPEC = pl.BlockSpec(memory_space=pl.ANY)
+HBM_SPEC = pl.BlockSpec(memory_space=pltpu.HBM)
 
 
 def local_call(kernel, name, flops, mebibytes, **kwargs):
@@ -588,11 +647,11 @@
     )
 
 
-def remote_call(kernel, name, identity, **kwargs):
+def remote_call(kernel, name, identity, mebibytes=24, **kwargs):
     return pl.pallas_call(
         kernel,
         compiler_params=pltpu.CompilerParams(
-            collective_id=identity, has_side_effects=True, vmem_limit_bytes=24 * 2**20
+            collective_id=identity, has_side_effects=True, vmem_limit_bytes=mebibytes * 2**20
         ),
         name=name,
         **kwargs,
@@ -621,57 +680,58 @@
     big = [pltpu.VMEM(square, BF16)] * 2
     thin = [pltpu.VMEM(tall, BF16)] * 2
 
-    pivot = remote_call(
-        gather_kernel, "gather_pivot", 1,
-        out_shape=shape_of(*square), in_specs=[ANY_SPEC], out_specs=ANY_SPEC,
-        scratch_shapes=[pltpu.SemaphoreType.DMA, dma_sems(COPIES), dma_sems(COPIES)],
-    )(diag_blocks)
+    pivot, arrow_full = remote_call(
+        gather_kernel, "gather_pivot", 1, 58,
+        out_shape=[shape_of(*square), shape_of(1, effects, order)],
+        in_specs=[HBM_SPEC] * 2, out_specs=[ANY_SPEC] * 2,
+        scratch_shapes=[dma_sems(2), dma_sems(COPIES + 1), dma_sems(COPIES + 1)],
+    )(diag_blocks, arrow_blocks)
     sub_full = lax.all_gather(sub_blocks, "blk", axis=2, tiled=True)
-    arrow_full = lax.all_gather(arrow_blocks, "blk", axis=2, tiled=True)
     inverse, log_first = inverse_and_log(pivot)
 
     packed_shape = shape_of(packed_rows, BLOCK)
-    swap, lower, upper, x_high, x_low = local_call(
-        first_products_kernel, "first_products", 10 * order**3, 44,
-        grid=(1,),
-        out_shape=[packed_shape] * 3 + [shape_of(*tall, dtype=BF16)] * 2,
-        in_specs=[SMEM_SPEC, *vmem(3), whole((1, *tall), (1, 0, 0)), whole((1, effects, half), (1, 0, 0))],
-        out_specs=vmem(5),
-        scratch_shapes=big * 3 + thin,
-    )(info, inverse, sub_full, arrow_full, diag_blocks, arrow_blocks)
+    packed_scratch = pltpu.VMEM((packed_rows, BLOCK), F32)
+    swap, rest, x_high, x_low = local_call(
+        first_products_kernel, "first_products", 10 * order**3, 58,
+        out_shape=[packed_shape] * 2 + [shape_of(*tall, dtype=BF16)] * 2,
+        in_specs=[SMEM_SPEC, *vmem(1), *[ANY_SPEC] * 4],
+        out_specs=vmem(4),
+        scratch_shapes=[pltpu.VMEM(square, F32)] * 3
+        + [pltpu.VMEM(tall, F32), pltpu.VMEM((effects, half), F32), dma_sems(5)]
+        + big * 3
+        + thin,
+    )(info, arrow_full, inverse, sub_full, diag_blocks, arrow_blocks)
     pairs = [(p, p + 1) for p in evens]
-    other = lax.ppermute(swap, "tm", pairs + [(b, a) for a, b in pairs])
-    left_own, tip_first = local_call(
-        first_fill_kernel, "first_fill", 3 * order**3, 32,
-        grid=(1,),
-        out_shape=[shape_of(*tall), shape_of(effects, effects)],
-        in_specs=[SMEM_SPEC, *vmem(1), whole((1, *square), (1, 0, 0)), whole((1, effects, order), (0, 0, 0)), *vmem(2)],
-        out_specs=vmem(2),
-        scratch_shapes=big,
-    )(info, inverse, sub_full, arrow_full, x_high, x_low)
-    lower_above = lax.ppermute(lower, "tm", down)
+    both, left_own, tip_first = remote_call(
+        pair_kernel, "swap_and_fill", 2, 58,
+        out_shape=[shape_of(2, packed_rows, BLOCK), shape_of(*tall), shape_of(effects, effects)],
+        in_specs=[ANY_SPEC] * 6,
+        out_specs=[ANY_SPEC, *vmem(2)],
+        scratch_shapes=[packed_scratch] * 3
+        + [pltpu.VMEM(square, F32)] * 2
+        + [pltpu.VMEM((effects, order), F32)]
+        + thin
+        + big
+        + [dma_sems(6), dma_sems(COPIES), dma_sems(COPIES), dma_sems(COPIES), dma_sems(COPIES), dma_sems(COPIES)],
+    )(swap, inverse, sub_full, arrow_full, x_high, x_low)
+    lower_above = lax.ppermute(rest, "tm", down)
     left_pair = lax.ppermute(left_own, "tm", pairs)
     left_full = lax.all_gather(left_own, "blk", axis=1, tiled=True)
 
-    both = remote_call(
-        combine_kernel, "gather_separator", 2,
-        out_shape=shape_of(2, packed_rows, BLOCK), in_specs=vmem(3), out_specs=ANY_SPEC,
-        scratch_shapes=[
-            pltpu.VMEM((packed_rows, BLOCK), F32),
-            pltpu.SemaphoreType.DMA, dma_sems(COPIES), dma_sems(COPIES),
-        ],
-    )(other, upper, lower)
     inverse, log_second, separator = inverse_of_packed(info, both, order, half)
     product = local_call(
-        second_products_kernel, "second_products", 5 * order**3, 40,
+        second_products_kernel, "second_products", 5 * order**3, 58,
         out_shape=packed_shape,
-        in_specs=[SMEM_SPEC, *vmem(5)],
+        in_specs=[SMEM_SPEC, *[ANY_SPEC] * 5],
         out_specs=vmem(1)[0],
-        scratch_shapes=big * 2 + thin,
-    )(info, inverse, left_full, both, upper, lower_above)
+        scratch_shapes=[pltpu.VMEM(square, F32)] * 2
+        + [pltpu.VMEM((2, packed_rows - PACKED * BLOCK, BLOCK), F32), packed_scratch, packed_scratch, dma_sems(5)]
+        + big * 2
+        + thin,
+    )(info, inverse, left_full, both, rest, lower_above)
     above = lax.ppermute(product, "tm", down)
     left_result, sums = local_call(
-        second_fill_kernel, "second_fill", 6 * order**3, 44,
+        second_fill_kernel, "second_fill", 6 * order**3, 58,
         out_shape=[shape_of(1, *tall), shape_of(effects + 8, TILE)],
         in_specs=[SMEM_SPEC, *vmem(8)],
         out_specs=vmem(2),

time: 253 us -> 298 us (1.18); the launches traced: 252 us -> 294 us
  Pallas kernels: 182 us -> 261 us
  waiting for transfers between devices: 30.3 us -> 0.71 us
  local copies, waits for them, and re-layouts: 17.5 us -> 10.9 us
    pallas_call x6 -> x5, Pallas kernels: 72.7 us -> 160 us  [the longest x1 68.8 us: on_device(): remote_call(gather_kernel, 'gather_pivot', 1, 58, out_shape=[shape_of(*sq...]
    ppermute x2 -> x1, waiting for transfers between devices: 29.6 us -> 0.01 us  [on_device(): lower_above = lax.ppermute(rest, 'tm', down)]
    unnamed x38 -> x22, local copies, waits for them, and re-layouts: 17.5 us -> 9.94 us
    pallas_call x1, Pallas kernels: 33.1 us -> 28 us  [on_device(): remote_call(functools.partial(reduce_kernel, sides), 'reduce_terms', 3, o...]
  transfers between devices with their start and end apart: 6 -> 5, of which waited for: 1 -> 0; matrix products, arithmetic and copies ran while one was open for 1% -> 1% of each run, Pallas kernels for 56% -> 67%
where the time goes in v1:
time: 298 us; the launch traced here: 294 us
  Pallas kernels  261 us (88%)
  between operations  14.2 us (5%)
  local copies, waits for them, and re-layouts  10.9 us (4%)
  starting transfers between devices  4.13 us (1%)
    pallas_call x1, Pallas kernels, on_device(): remote_call(gather_kernel, 'gather_pivot', 1, 58, out_shape=[shape_of(*sq...  68.8 us
    pallas_call x1, Pallas kernels, on_device(): remote_call(pair_kernel, 'swap_and_fill', 2, 58, out_shape=[shape_of(2, p...  37.2 us
    pallas_call x1, Pallas kernels, inverse_of_packed(): local_call(packed_inverse_kernel, 'second_inverse', 24 * order ** 3, 20,...  34.1 us
    pallas_call x1, Pallas kernels, inverse_and_log(): local_call(inverse_kernel, 'first_inverse', 24 * order ** 3, 16, out_shap...  33.8 us
    pallas_call x1, Pallas kernels, on_device(): remote_call(functools.partial(reduce_kernel, sides), 'reduce_terms', 3, o...  28 us
    pallas_call x1, Pallas kernels, on_device(): local_call(first_products_kernel, 'first_products', 10 * order ** 3, 58,...  22.7 us
    pallas_call x1, Pallas kernels, on_device(): local_call(second_fill_kernel, 'second_fill', 6 * order ** 3, 58, out_sha...  17.1 us
    pallas_call x1, Pallas kernels, on_device(): local_call(second_products_kernel, 'second_products', 5 * order ** 3, 58,...  13.8 us
  transfers between devices with their start and end apart: 5, of which 0 were waited for; matrix products, arithmetic and copies ran while one was open for 1% of the time, Pallas kernels for 67%

profile of v1, /device:TPU:25, one launch (start us, length us, event | category | flops | bytes accessed | tf_op | source)
XLA Modules:
  0.0 293.9 jit_solution(7190583116068091181)
XLA Ops:
  7.2 0.7 all-gather.3.cloned.1.call-update
  8.0 68.8 %gather_pivot.1 = (f32[1024,1024]{1,0:T(8,128)}, f32[1,64,1024]{2,1,0:T(8,128)}) custom-call(f32[2,1024,512]{2,1,0:T(8,128)} %diag_hbm.1, f32[2,64,512]{2,1,0:T(8,128)} %own_arrow_hbm.1), custom_call_target="tpu_custom_call" | custom-call | tf_op jit(solution)/shard_map/gather_pivot/pallas_call | solution.py:683
  76.8 0.6 pad_add_fusion.info_ref
  77.4 2.2 copy-done.6
  79.6 33.8 %first_inverse.1 = (f32[1024,1024]{1,0:T(8,128)S(1)}, f32[8,128]{1,0:T(8,128)S(1)}) custom-call(f32[1024,1024]{1,0:T(8,128)S(1)} %copy-done.6), custom_call_target="tpu_custom_call" | custom-call | flops 25769803776 | bytes 8388608 | tf_op jit(solution)/shard_map/first_inverse/pallas_call | solution.py:212
  113.4 2.0 copy-done
  116.0 22.7 %first_products.1 = (f32[1408,256]{1,0:T(8,128)}, f32[1408,256]{1,0:T(8,128)}, bf16[1024,512]{1,0:T(8,128)(2,1)}, bf16[1024,512]{1,0:T(8,128)(2,1)}) custom-call(s32[3]{0:T(128)} %pad_add_fusion.info_ref, f32[1,64,1024]{2,1,0:T(8,128)} %get-tuple-element.23.arrow_ref.arrow_hbm, f32[1024,1024]{1,0:T(8,128)} %copy-done, ...), custom_call_target="tpu_custom_call" | custom-call | flops 10737418240 | bytes 8388608 | tf_op jit(solution)/shard_map/first_products/pallas_call | solution.py:694
  138.7 37.2 %swap_and_fill.1 = (f32[2,1408,256]{2,1,0:T(8,128)}, f32[1024,512]{1,0:T(8,128)}, f32[64,64]{1,0:T(8,128)}) custom-call(f32[1408,256]{1,0:T(8,128)} %get-tuple-element.26.swap_hbm, f32[1024,1024]{1,0:T(8,128)} %copy-done, f32[2,1024,1024]{2,1,0:T(8,128)} %all-gather.3.cloned.1.call-done.sub_hbm, f32[1,64,1024]{2,1,0:T(8,128)} %get-tuple-element.23.arrow_ref.arrow_hbm, ...), custom_call_target="tpu_custom_call" | custom-call | tf_op jit(solution)/shard_map/swap_and_fill/pallas_call | solution.py:705
  175.9 1.3 collective-permute-start.2
  177.2 1.5 collective-permute-start
  178.7 1.8 copy-done.3
  180.5 34.1 %second_inverse.1 = (f32[1024,1024]{1,0:T(8,128)S(1)}, f32[8,128]{1,0:T(8,128)S(1)}, f32[1024,512]{1,0:T(8,128)S(1)}) custom-call(s32[3]{0:T(128)S(1)} %copy-done.4, f32[2,1408,256]{2,1,0:T(8,128)S(1)} %copy-done.3), custom_call_target="tpu_custom_call" | custom-call | flops 25769803776 | bytes 8388608 | tf_op jit(solution)/shard_map/second_inverse/pallas_call | solution.py:220
  214.6 2.0 copy-done.7
  217.2 13.8 %second_products.1.kept_ref = f32[1408,256]{1,0:T(8,128)} custom-call(s32[3]{0:T(128)} %pad_add_fusion.info_ref, f32[1024,1024]{1,0:T(8,128)} %copy-done.7, f32[1024,1024]{1,0:T(8,128)} %all-gather.5.cloned.1.call-done.left_hbm.left_ref, f32[2,1408,256]{2,1,0:T(8,128)} %get-tuple-element.29.both_ref.both_hbm.sep_ref, ...), custom_call_target="tpu_custom_call" | custom-call | flops 5368709120 | bytes 8388608 | tf_op jit(solution)/shard_map/second_products/pallas_call | solution.py:722
  231.0 1.3 collective-permute-start.1
  232.4 1.0 slice.18
  233.4 17.1 %second_fill.1 = (f32[1,1024,512]{2,1,0:T(8,128)}, f32[72,128]{1,0:T(8,128)}) custom-call(s32[3]{0:T(128)} %pad_add_fusion.info_ref, f32[1024,1024]{1,0:T(8,128)} %copy-done.7, f32[1024,1024]{1,0:T(8,128)} %all-gather.5.cloned.1.call-done.left_hbm.left_ref, f32[2,1408,256]{2,1,0:T(8,128)} %get-tuple-element.29.both_ref.both_hbm.sep_ref, ...), custom_call_target="tpu_custom_call" | custom-call | flops 6442450944 | bytes 8388608 | tf_op jit(solution)/shard_map/second_fill/pallas_call | solution.py:733
  250.5 0.8 copy-done.2
  251.3 28.0 %reduce_terms.1 = f32[72,128]{1,0:T(8,128)S(1)} custom-call(f32[72,128]{1,0:T(8,128)S(1)} %copy-done.2), custom_call_target="tpu_custom_call" | custom-call | tf_op jit(solution)/shard_map/reduce_terms/pallas_call | solution.py:741
  279.2 0.6 slice_reduce_fusion
  279.8 0.6 slice_subtract_fusion
  280.5 3.7 %finish_blocks.1 = (f32[1408,256]{1,0:T(8,128)S(1)}, f32[512,256]{1,0:T(8,128)S(1)}) custom-call(f32[1408,256]{1,0:T(8,128)S(1)} %copy-done.1, f32[1408,256]{1,0:T(8,128)S(1)} %collective-permute-done.1.above_ref), custom_call_target="tpu_custom_call" | custom-call | tf_op jit(solution)/shard_map/finish_blocks/pallas_call | solution.py:749
  284.2 2.2 place_blocks.1
  286.4 0.7 maximum_bitcast_fusion
  (27 shorter events, 1.3 us)
Async XLA Ops:
  7.2 108.8 %all-gather.3.cloned.1.call-start = ((), (), s32[]{:S(2)}) async-start(), calls=%async_computation | async-start | bytes 12582912 | tf_op jit(solution)/shard_map/all_gather | solution.py:689
  7.9 209.3 %all-gather.5.cloned.1.call-start = ((), (), s32[]{:S(2)}) async-start(), calls=%async_computation.1 | async-start | bytes 6291456 | tf_op jit(solution)/shard_map/all_gather | solution.py:719
  77.4 2.2 copy-start.6
  113.4 2.0 copy-start
  115.4 0.6 copy-start.8
  175.9 2.8 copy-start.4
  175.9 57.4 %collective-permute-start.2 = (f32[1024,512]{1,0:T(8,128)}, f32[1024,512]{1,0:T(8,128)}, u32[]{:S(2)}, u32[]{:S(2)}) collective-permute-start(f32[1024,512]{1,0:T(8,128)} %get-tuple-element.31.own_ref), channel_id=1, source_target_pairs={{0,2},{4,6},{8,10},{12,14},{16,18},{20,22},{24,26},{28,30},{32,34}... | collective-permute-start | bytes 6291464 | tf_op jit(solution)/shard_map/ppermute | solution.py:718
  177.2 40.0 %collective-permute-start = (f32[1408,256]{1,0:T(8,128)}, f32[1408,256]{1,0:T(8,128)}, u32[]{:S(2)}, u32[]{:S(2)}) collective-permute-start(f32[1408,256]{1,0:T(8,128)} %get-tuple-element.32.rest_hbm), channel_id=1, source_target_pairs={{4,2},{8,6},{12,10},{16,14},{20,18},{24,22},{28,26},{32,30},{36,34... | collective-permute-start | bytes 4325384 | tf_op jit(solution)/shard_map/ppermute | solution.py:717
  178.7 1.8 copy-start.3
  214.6 2.0 copy-start.7
  216.6 0.6 copy-start.9
  231.0 49.4 %collective-permute-start.1 = (f32[1408,256]{1,0:T(8,128)}, f32[1408,256]{1,0:T(8,128)S(1)}, u32[]{:S(2)}, u32[]{:S(2)}) collective-permute-start(f32[1408,256]{1,0:T(8,128)} %second_products.1.kept_ref), channel_id=1, source_target_pairs={{4,2},{8,6},{12,10},{16,14},{20,18},{24,22},{28,26},{32,30},{36,34... | collective-permute-start | bytes 4325384 | tf_op jit(solution)/shard_map/ppermute | solution.py:732
  233.3 46.5 %copy-start.10 = (f32[64,64]{1,0:T(8,128)S(1)}, f32[64,64]{1,0:T(8,128)}, u32[]{:S(2)}) copy-start(f32[64,64]{1,0:T(8,128)} %param.7) | copy-start | bytes 49156
  233.4 47.1 %copy-start.1 = (f32[1408,256]{1,0:T(8,128)S(1)}, f32[1408,256]{1,0:T(8,128)}, u32[]{:S(2)}) copy-start(f32[1408,256]{1,0:T(8,128)} %second_products.1.kept_ref) | copy-start | bytes 4325380
  250.5 33.7 %copy-start.5 = (s32[3]{0:T(128)S(1)}, s32[3]{0:T(128)}, u32[]{:S(2)}) copy-start(s32[3]{0:T(128)} %pad_add_fusion.info_ref) | copy-start | bytes 40
  250.5 0.8 copy-start.2
Sparse Core Ops, SparseCore 0:
  9.6 25.1 all-gather.2
  176.0 18.6 all-gather.4

commit v2 on v1

--- a/solution.py
+++ b/solution.py
@@ -13,6 +13,7 @@
 BLOCK = 256
 PACKED = 5
 COPIES = 4
+SIDE = 4
 GROUP = 2
 SLOTS = TILE // (8 * GROUP)
 
@@ -354,8 +355,8 @@
 
 
 def second_products_kernel(
-    info_ref, inverse_hbm, left_hbm, both_hbm, rest_hbm, above_hbm, out_ref,
-    inverse_ref, left_ref, arrow_ref, rest_ref, above_ref, sems, vh, vl, bh, bl, xh, xl,
+    info_ref, inverse_hbm, left_hbm, both_hbm, rest_hbm, out_ref,
+    inverse_ref, left_ref, arrow_ref, rest_ref, sems, vh, vl, bh, bl, xh, xl,
 ):
     core, even = info_ref[0], info_ref[1] == 1
     half = xh.shape[1]
@@ -367,7 +368,6 @@
             (left_hbm, left_ref),
             (both_hbm.at[:, pl.ds(PACKED * BLOCK, arrow_ref.shape[1]), :], arrow_ref),
             (rest_hbm, rest_ref),
-            (above_hbm, above_ref),
         ),
         sems,
     )
@@ -384,10 +384,10 @@
         solve_into((vh, vl), (bh[:, own], bl[:, own]), (xh, xl), 0)
 
         def store(k, row, column, value):
-            out_ref[block_span(k), :] = value
+            out_ref[block_span(k), :] = rest_ref[block_span(k), :] + value
 
         packed_gram(core, (bh, bl), (xh, xl), 0, store)
-        out_ref[last, :] = arrow_pack(times(rows, (xh[...], xl[...])))
+        out_ref[last, :] = rest_ref[last, :] + arrow_pack(times(rows, (xh[...], xl[...])))
 
     @pl.when(jnp.logical_not(even))
     def _():
@@ -395,32 +395,28 @@
 
         def store(k, row, column, value):
             span = block_span(k)
-            out_ref[span, :] = rest_ref[span, :] - above_ref[span, :] - value
+            out_ref[span, :] = rest_ref[span, :] - value
 
         packed_gram(core, (bh, bl), (xh, xl), 1, store)
         change = arrow_pack(times(rows, (xh[...], xl[...])))
-        out_ref[last, :] = rest_ref[last, :] - above_ref[last, :] - change
+        out_ref[last, :] = rest_ref[last, :] - change
 
 
 def second_fill_kernel(
-    info_ref, inverse_ref, left_ref, sep_ref, own_ref, pair_ref, tip_ref, log_ref, log_two_ref,
+    info_ref, inverse_ref, left_ref, sep_ref, own_ref, pair_ref, pair_sums_ref, log_ref,
     out_ref, sums_ref, vh, vl, bh, bl, xh, xl,
 ):
     even = info_ref[1] == 1
-    effects = tip_ref.shape[0]
-    sums_ref[...] = jnp.zeros_like(sums_ref)
 
     @pl.when(even)
     def _():
         out_ref[0] = own_ref[...]
-        tip = tip_ref[...] + arrow_form(separator_arrow(sep_ref[:, PACKED * BLOCK :, :]), inverse_ref)
-        sums_ref[0:effects, 0:effects] = tip
-        sums_ref[effects:, :] = log_ref[...] + log_two_ref[...]
+        sums_ref[...] = pair_sums_ref[...]
 
     @pl.when(jnp.logical_not(even))
     def _():
-        sums_ref[0:effects, 0:effects] = tip_ref[...]
-        sums_ref[effects:, :] = log_ref[...]
+        put_sums(sums_ref, arrow_form(separator_arrow(sep_ref[:, PACKED * BLOCK :, :]), inverse_ref), log_ref[...])
+        sums_ref[...] = sums_ref[...] + pair_sums_ref[...]
         split_rows(inverse_ref, vh, vl, -1)
         split_rows(left_ref, bh, bl)
         solve_into((vh, vl), split_two(pair_ref[...]), (xh, xl), 0)
@@ -478,10 +474,17 @@
         copy.wait()
 
 
+def put_sums(sums_ref, tip, logs):
+    effects = tip.shape[0]
+    sums_ref[...] = jnp.zeros_like(sums_ref)
+    sums_ref[0:effects, 0:effects] = tip
+    sums_ref[effects:, :] = logs
+
+
 def pair_kernel(
-    swap_hbm, inverse_hbm, sub_hbm, arrow_hbm, xh_hbm, xl_hbm, both_hbm, left_ref, tip_ref,
-    own_ref, other_ref, sum_ref, inverse_ref, right_ref, arrow_ref, xh, xl, sh, sl,
-    sems, local_sems, swap_send, swap_recv, send_sem, recv_sem,
+    swap_hbm, inverse_hbm, sub_hbm, arrow_hbm, xh_hbm, xl_hbm, log_ref, both_hbm, left_ref, pair_sums_ref,
+    own_ref, other_ref, sum_ref, own_sums_ref, other_sums_ref, inverse_ref, right_ref, arrow_ref, xh, xl, sh, sl,
+    sems, local_sems, swap_send, swap_recv, send_sem, recv_sem, sums_send, sums_recv,
 ):
     core, me = lax.axis_index("blk"), lax.axis_index("tm")
     even = me % 2 == 0
@@ -514,7 +517,8 @@
         return carry
 
     lax.fori_loop(0, sh.shape[0] // BLOCK, part, 0)
-    tip_ref[...] = arrow_form(arrow_ref[...], inverse_ref)
+    put_sums(own_sums_ref, arrow_form(arrow_ref[...], inverse_ref), log_ref[...])
+    sums = exchange([(own_sums_ref, other_sums_ref)], partner, sums_send, sums_recv)
     shares = []
     for k, span in enumerate(spans):
         swaps[k].wait()
@@ -526,8 +530,9 @@
         shares += exchange(
             [(sum_ref.at[span, :], both_hbm.at[core, span, :])], peer, send_sem.at[pl.ds(k, 1)], recv_sem.at[pl.ds(k, 1)]
         )
-    for copy in shares:
+    for copy in shares + sums:
         copy.wait()
+    pair_sums_ref[...] = own_sums_ref[...] + other_sums_ref[...]
 
 
 def finish_kernel(kept_ref, above_ref, out_ref, peer_ref, send_sem, recv_sem):
@@ -585,43 +590,54 @@
             put(row, column, value)
 
 
-def reduce_kernel(sides, value_ref, out_ref, parts_ref, send_sem, recv_sem):
+def reduce_kernel(side, value_ref, out_ref, parts_ref, send_sem, recv_sem, last_send, last_recv):
     me = lax.axis_index("tm")
-    stages = []
-    stride = 1
-    for side in reversed(sides):
-        place = (me // stride) % side
-        stages.append((side, place, stride))
-        stride = stride * side
+    odd = me % 2 == 1
+    stages = [(side, (me // side) % side, side), (side, (me // side**2) % side, side**2), (2, (me // 2) % 2, 2)]
 
     def other(stage, step):
-        side, place, stride = stages[stage]
-        return me + ((place + step) % side - place) * stride
-
-    meet([{"tm": other(s, d)} for s in range(len(stages)) for d in range(1, stages[s][0])])
-    out_ref[...] = value_ref[...]
-    for s in reversed(range(len(stages))):
-        side, place, _ = stages[s]
-        parts_ref[s, place] = out_ref[...]
-        copies = []
-        for d in range(1, side):
-            copies.append(
-                pltpu.make_async_remote_copy(
-                    src_ref=out_ref,
-                    dst_ref=parts_ref.at[s, place],
-                    send_sem=send_sem.at[s, d],
-                    recv_sem=recv_sem.at[s, d],
-                    device_id={"tm": other(s, d)},
-                    device_id_type=pl.DeviceIdType.MESH,
+        count, place, stride = stages[stage]
+        return me + ((place + step) % count - place) * stride
+
+    def hand(partner):
+        return pltpu.make_async_remote_copy(
+            src_ref=out_ref,
+            dst_ref=out_ref,
+            send_sem=last_send,
+            recv_sem=last_recv,
+            device_id={"tm": partner},
+            device_id_type=pl.DeviceIdType.MESH,
+        )
+
+    @pl.when(odd)
+    def _():
+        others = [{"tm": other(s, d)} for s in range(len(stages)) for d in range(1, stages[s][0])]
+        meet(others + [{"tm": me - 1}])
+        out_ref[...] = value_ref[...]
+        for s, (count, place, _) in enumerate(stages):
+            parts_ref[s, place] = out_ref[...]
+            copies = []
+            for d in range(1, count):
+                copies += exchange(
+                    [(out_ref, parts_ref.at[s, place])],
+                    {"tm": other(s, d)},
+                    send_sem.at[s, pl.ds(d, 1)],
+                    recv_sem.at[s, pl.ds(d, 1)],
                 )
-            )
-            copies[-1].start()
-        for copy in copies:
-            copy.wait()
-        total = parts_ref[s, 0]
-        for k in range(1, side):
-            total = total + parts_ref[s, k]
-        out_ref[...] = total
+            for copy in copies:
+                copy.wait()
+            total = parts_ref[s, 0]
+            for k in range(1, count):
+                total = total + parts_ref[s, k]
+            out_ref[...] = total
+        copy = hand(me - 1)
+        copy.start()
+        copy.wait_send()
+
+    @pl.when(jnp.logical_not(odd))
+    def _():
+        meet([{"tm": me + 1}])
+        hand(me + 1).wait_recv()
 
 
 def vmem(count):
@@ -681,7 +697,7 @@
     thin = [pltpu.VMEM(tall, BF16)] * 2
 
     pivot, arrow_full = remote_call(
-        gather_kernel, "gather_pivot", 1, 58,
+        gather_kernel, "gather_pivot", 1,
         out_shape=[shape_of(*square), shape_of(1, effects, order)],
         in_specs=[HBM_SPEC] * 2, out_specs=[ANY_SPEC] * 2,
         scratch_shapes=[dma_sems(2), dma_sems(COPIES + 1), dma_sems(COPIES + 1)],
@@ -702,19 +718,19 @@
         + thin,
     )(info, arrow_full, inverse, sub_full, diag_blocks, arrow_blocks)
     pairs = [(p, p + 1) for p in evens]
-    both, left_own, tip_first = remote_call(
+    both, left_own, pair_sums = remote_call(
         pair_kernel, "swap_and_fill", 2, 58,
-        out_shape=[shape_of(2, packed_rows, BLOCK), shape_of(*tall), shape_of(effects, effects)],
-        in_specs=[ANY_SPEC] * 6,
+        out_shape=[shape_of(2, packed_rows, BLOCK), shape_of(*tall), shape_of(effects + 8, TILE)],
+        in_specs=[*[ANY_SPEC] * 6, *vmem(1)],
         out_specs=[ANY_SPEC, *vmem(2)],
         scratch_shapes=[packed_scratch] * 3
+        + [pltpu.VMEM((effects + 8, TILE), F32)] * 2
         + [pltpu.VMEM(square, F32)] * 2
         + [pltpu.VMEM((effects, order), F32)]
         + thin
         + big
-        + [dma_sems(6), dma_sems(COPIES), dma_sems(COPIES), dma_sems(COPIES), dma_sems(COPIES), dma_sems(COPIES)],
-    )(swap, inverse, sub_full, arrow_full, x_high, x_low)
-    lower_above = lax.ppermute(rest, "tm", down)
+        + [dma_sems(6), *[dma_sems(COPIES)] * 5, dma_sems(1), dma_sems(1)],
+    )(swap, inverse, sub_full, arrow_full, x_high, x_low, log_first)
     left_pair = lax.ppermute(left_own, "tm", pairs)
     left_full = lax.all_gather(left_own, "blk", axis=1, tiled=True)
 
@@ -722,28 +738,27 @@
     product = local_call(
         second_products_kernel, "second_products", 5 * order**3, 58,
         out_shape=packed_shape,
-        in_specs=[SMEM_SPEC, *[ANY_SPEC] * 5],
+        in_specs=[SMEM_SPEC, *[ANY_SPEC] * 4],
         out_specs=vmem(1)[0],
         scratch_shapes=[pltpu.VMEM(square, F32)] * 2
-        + [pltpu.VMEM((2, packed_rows - PACKED * BLOCK, BLOCK), F32), packed_scratch, packed_scratch, dma_sems(5)]
+        + [pltpu.VMEM((2, packed_rows - PACKED * BLOCK, BLOCK), F32), packed_scratch, dma_sems(4)]
         + big * 2
         + thin,
-    )(info, inverse, left_full, both, rest, lower_above)
+    )(info, inverse, left_full, both, rest)
     above = lax.ppermute(product, "tm", down)
     left_result, sums = local_call(
         second_fill_kernel, "second_fill", 6 * order**3, 58,
         out_shape=[shape_of(1, *tall), shape_of(effects + 8, TILE)],
-        in_specs=[SMEM_SPEC, *vmem(8)],
+        in_specs=[SMEM_SPEC, *vmem(7)],
         out_specs=vmem(2),
         scratch_shapes=big * 2 + thin,
-    )(info, inverse, left_full, both, left_own, left_pair, tip_first, log_first, log_second)
-    sides = side_lengths(parts)
+    )(info, inverse, left_full, both, left_own, left_pair, pair_sums, log_second)
     totals = remote_call(
-        functools.partial(reduce_kernel, sides), "reduce_terms", 3,
+        functools.partial(reduce_kernel, SIDE), "reduce_terms", 3,
         out_shape=shape_of(effects + 8, TILE), in_specs=vmem(1), out_specs=vmem(1)[0],
         scratch_shapes=[
-            pltpu.VMEM((len(sides), max(sides), effects + 8, TILE), F32),
-            dma_sems(len(sides), max(sides)), dma_sems(len(sides), max(sides)),
+            pltpu.VMEM((3, SIDE, effects + 8, TILE), F32),
+            dma_sems(3, SIDE), dma_sems(3, SIDE), pltpu.SemaphoreType.DMA, pltpu.SemaphoreType.DMA,
         ],
     )(sums)
     packed, swapped = remote_call(
@@ -767,15 +782,6 @@
     )
 
 
-def side_lengths(parts):
-    sides = []
-    while parts > 1:
-        side = 4 if parts % 4 == 0 else parts
-        sides.append(side)
-        parts //= side
-    return tuple(sides)
-
-
 def solution(mesh):
     in_specs = (P("tm", None, "blk"), P("tm", None, "blk"), P("tm", None, "blk"), P())
     out_specs = (P("tm", None, "blk"), P("tm", None, "blk"), P("tm", None, "blk"), P(), P())

time: 298 us -> 232 us (0.78)
  the two profiles are of different devices: /device:TPU:25 before, /device:TPU:39 now
where the time goes in v2:
time: 232 us; the launch traced here: 231 us
  Pallas kernels  196 us (84%)
  between operations  14.2 us (6%)
  local copies, waits for them, and re-layouts  11.8 us (5%)
  starting transfers between devices  6.08 us (3%)
  other arithmetic  2.56 us (1%)
    pallas_call x1, Pallas kernels, on_device(): remote_call(pair_kernel, 'swap_and_fill', 2, 58, out_shape=[shape_of(2, p...  38.4 us
    pallas_call x1, Pallas kernels, inverse_of_packed(): local_call(packed_inverse_kernel, 'second_inverse', 24 * order ** 3, 20,...  34.1 us
    pallas_call x1, Pallas kernels, inverse_and_log(): local_call(inverse_kernel, 'first_inverse', 24 * order ** 3, 16, out_shap...  33.8 us
    pallas_call x1, Pallas kernels, on_device(): remote_call(functools.partial(reduce_kernel, SIDE), 'reduce_terms', 3, ou...  33.3 us
    pallas_call x1, Pallas kernels, on_device(): local_call(first_products_kernel, 'first_products', 10 * order ** 3, 58,...  22.7 us
    pallas_call x1, Pallas kernels, on_device(): local_call(second_products_kernel, 'second_products', 5 * order ** 3, 58,...  14.3 us
    unnamed x26, local copies, waits for them, and re-layouts  10.8 us
    pallas_call x1, Pallas kernels, on_device(): local_call(second_fill_kernel, 'second_fill', 6 * order ** 3, 58, out_sha...  7.3 us
  transfers between devices with their start and end apart: 4, of which 0 were waited for; matrix products, arithmetic and copies ran while one was open for 1% of the time, Pallas kernels for 55%

profile of v2, /device:TPU:39, one launch (start us, length us, event | category | flops | bytes accessed | tf_op | source)
XLA Modules:
  0.0 231.2 jit_solution(4929484343822008443)
XLA Ops:
  7.2 0.7 all-gather.3.cloned.1.call-update
  8.1 2.2 copy-done.1
  10.3 5.2 %gather_pivot.1 = (f32[1024,1024]{1,0:T(8,128)S(1)}, f32[1,64,1024]{2,1,0:T(8,128)S(1)}) custom-call(f32[2,1024,512]{2,1,0:T(8,128)S(1)} %copy-done.1, f32[2,64,512]{2,1,0:T(8,128)S(1)} %copy-done.4), custom_call_target="tpu_custom_call" | custom-call | tf_op jit(solution)/shard_map/gather_pivot/pallas_call | solution.py:699
  15.5 0.7 copy-done.3
  16.2 0.7 pad_add_fusion.info_ref
  16.8 33.8 %first_inverse.1 = (f32[1024,1024]{1,0:T(8,128)S(1)}, f32[8,128]{1,0:T(8,128)S(1)}) custom-call(f32[1024,1024]{1,0:T(8,128)S(1)} %get-tuple-element.24.source_ref), custom_call_target="tpu_custom_call" | custom-call | flops 25769803776 | bytes 8388608 | tf_op jit(solution)/shard_map/first_inverse/pallas_call | solution.py:213
  50.6 2.0 copy-done
  53.2 22.7 %first_products.1 = (f32[1408,256]{1,0:T(8,128)}, f32[1408,256]{1,0:T(8,128)}, bf16[1024,512]{1,0:T(8,128)(2,1)}, bf16[1024,512]{1,0:T(8,128)(2,1)}) custom-call(s32[3]{0:T(128)} %pad_add_fusion.info_ref, f32[1,64,1024]{2,1,0:T(8,128)} %copy-done.3, f32[1024,1024]{1,0:T(8,128)} %copy-done, f32[2,1024,1024]{2,1,0:T(8,128)} %all-gather.3.cloned.1.call-done.sub_hbm, ...), custom_call_target="tpu_custom_call" | custom-call | flops 10737418240 | bytes 8388608 | tf_op jit(solution)/shard_map/first_products/pallas_call | solution.py:710
  75.9 38.4 %swap_and_fill.1 = (f32[2,1408,256]{2,1,0:T(8,128)}, f32[1024,512]{1,0:T(8,128)}, f32[72,128]{1,0:T(8,128)}) custom-call(f32[1408,256]{1,0:T(8,128)} %get-tuple-element.26.swap_hbm, f32[1024,1024]{1,0:T(8,128)} %copy-done, f32[2,1024,1024]{2,1,0:T(8,128)} %all-gather.3.cloned.1.call-done.sub_hbm, f32[1,64,1024]{2,1,0:T(8,128)} %copy-done.3, ...), custom_call_target="tpu_custom_call" | custom-call | tf_op jit(solution)/shard_map/swap_and_fill/pallas_call | solution.py:721
  114.4 4.6 %collective-permute-start.1 = (f32[1024,512]{1,0:T(8,128)}, f32[1024,512]{1,0:T(8,128)}, u32[]{:S(2)}, u32[]{:S(2)}) collective-permute-start(f32[1024,512]{1,0:T(8,128)} %get-tuple-element.32.own_ref), channel_id=1, source_target_pairs={{0,2},{4,6},{8,10},{12,14},{16,18},{20,22},{24,26},{28,30},{32,34}... | collective-permute-start | bytes 6291464 | tf_op jit(solution)/shard_map/ppermute | solution.py:734
  119.0 1.8 copy-done.6
  120.8 34.1 %second_inverse.1 = (f32[1024,1024]{1,0:T(8,128)S(1)}, f32[8,128]{1,0:T(8,128)S(1)}, f32[1024,512]{1,0:T(8,128)S(1)}) custom-call(s32[3]{0:T(128)S(1)} %copy-done.8, f32[2,1408,256]{2,1,0:T(8,128)S(1)} %copy-done.6), custom_call_target="tpu_custom_call" | custom-call | flops 25769803776 | bytes 8388608 | tf_op jit(solution)/shard_map/second_inverse/pallas_call | solution.py:221
  154.9 2.0 copy-done.10
  157.5 14.3 %second_products.1.kept_ref = f32[1408,256]{1,0:T(8,128)} custom-call(s32[3]{0:T(128)} %pad_add_fusion.info_ref, f32[1024,1024]{1,0:T(8,128)} %copy-done.10, f32[1024,1024]{1,0:T(8,128)} %all-gather.5.cloned.1.call-done.left_hbm.left_ref, f32[2,1408,256]{2,1,0:T(8,128)} %get-tuple-element.30.both_ref.both_hbm.sep_ref, f32[1408,256]{1,0:T(8,128)} %get-tuple-element.33.rest_hbm), custom_call_target="tpu_custom_call" | custom-call | flops 5368709120 | bytes 8388608 | tf_op jit(solution)/shard_map/second_products/pallas_call | solution.py:738
  171.9 1.4 collective-permute-start
  173.3 1.0 slice.18
  174.3 7.3 %second_fill.1 = (f32[1,1024,512]{2,1,0:T(8,128)}, f32[72,128]{1,0:T(8,128)}) custom-call(s32[3]{0:T(128)} %pad_add_fusion.info_ref, f32[1024,1024]{1,0:T(8,128)} %copy-done.10, f32[1024,1024]{1,0:T(8,128)} %all-gather.5.cloned.1.call-done.left_hbm.left_ref, f32[2,1408,256]{2,1,0:T(8,128)} %get-tuple-element.30.both_ref.both_hbm.sep_ref, ...), custom_call_target="tpu_custom_call" | custom-call | flops 6442450944 | bytes 8388608 | tf_op jit(solution)/shard_map/second_fill/pallas_call | solution.py:749
  181.6 0.8 copy-done.5
  182.3 33.3 %reduce_terms.1 = f32[72,128]{1,0:T(8,128)S(1)} custom-call(f32[72,128]{1,0:T(8,128)S(1)} %copy-done.5), custom_call_target="tpu_custom_call" | custom-call | tf_op jit(solution)/shard_map/reduce_terms/pallas_call | solution.py:756
  215.6 0.6 slice_reduce_fusion
  216.2 0.6 slice_subtract_fusion
  216.9 4.7 %finish_blocks.1 = (f32[1408,256]{1,0:T(8,128)S(1)}, f32[512,256]{1,0:T(8,128)S(1)}) custom-call(f32[1408,256]{1,0:T(8,128)S(1)} %copy-done.2, f32[1408,256]{1,0:T(8,128)S(1)} %collective-permute-done.above_ref), custom_call_target="tpu_custom_call" | custom-call | tf_op jit(solution)/shard_map/finish_blocks/pallas_call | solution.py:764
  221.7 2.0 place_blocks.1
  223.7 0.7 maximum_bitcast_fusion
  (29 shorter events, 1.5 us)
Async XLA Ops:
  7.2 1.0 copy-start.4
  7.2 46.0 %all-gather.3.cloned.1.call-start = ((), (), s32[]{:S(2)}) async-start(), calls=%async_computation | async-start | bytes 12582912 | tf_op jit(solution)/shard_map/all_gather | solution.py:705
  7.9 149.6 %all-gather.5.cloned.1.call-start = ((), (), s32[]{:S(2)}) async-start(), calls=%async_computation.1 | async-start | bytes 6291456 | tf_op jit(solution)/shard_map/all_gather | solution.py:735
  8.1 2.2 copy-start.1
  15.5 0.7 copy-start.3
  50.6 2.0 copy-start
  52.6 0.6 copy-start.7
  114.3 4.7 %copy-start.8 = (s32[3]{0:T(128)S(1)}, s32[3]{0:T(128)}, u32[]{:S(2)}) copy-start(s32[3]{0:T(128)} %pad_add_fusion.info_ref) | copy-start | bytes 40
  114.4 59.9 %collective-permute-start.1 = (f32[1024,512]{1,0:T(8,128)}, f32[1024,512]{1,0:T(8,128)}, u32[]{:S(2)}, u32[]{:S(2)}) collective-permute-start(f32[1024,512]{1,0:T(8,128)} %get-tuple-element.32.own_ref), channel_id=1, source_target_pairs={{0,2},{4,6},{8,10},{12,14},{16,18},{20,22},{24,26},{28,30},{32,34}... | collective-permute-start | bytes 6291464 | tf_op jit(solution)/shard_map/ppermute | solution.py:734
  119.0 1.8 copy-start.6
  154.9 2.0 copy-start.10
  157.0 0.6 copy-start.11
  171.9 45.0 %collective-permute-start = (f32[1408,256]{1,0:T(8,128)}, f32[1408,256]{1,0:T(8,128)S(1)}, u32[]{:S(2)}, u32[]{:S(2)}) collective-permute-start(f32[1408,256]{1,0:T(8,128)} %second_products.1.kept_ref), channel_id=1, source_target_pairs={{4,2},{8,6},{12,10},{16,14},{20,18},{24,22},{28,26},{32,30},{36,34... | collective-permute-start | bytes 4325384 | tf_op jit(solution)/shard_map/ppermute | solution.py:748
  174.2 42.0 %copy-start.12 = (f32[64,64]{1,0:T(8,128)S(1)}, f32[64,64]{1,0:T(8,128)}, u32[]{:S(2)}) copy-start(f32[64,64]{1,0:T(8,128)} %param.7) | copy-start | bytes 49156
  174.3 42.6 %copy-start.2 = (f32[1408,256]{1,0:T(8,128)S(1)}, f32[1408,256]{1,0:T(8,128)}, u32[]{:S(2)}) copy-start(f32[1408,256]{1,0:T(8,128)} %second_products.1.kept_ref) | copy-start | bytes 4325380
  181.6 40.1 %copy-start.9 = (s32[3]{0:T(128)S(1)}, s32[3]{0:T(128)}, u32[]{:S(2)}) copy-start(s32[3]{0:T(128)} %pad_add_fusion.info_ref) | copy-start | bytes 40
  181.6 0.8 copy-start.5
Sparse Core Ops, SparseCore 0:
  9.7 25.0 all-gather.2
  114.5 18.1 all-gather.4
